TPU v7x, 32 devices: a whole 2x2x4 slice. The times are simulated.
32 devices in a mesh: ctx: 16 (over z, x, core), head: 2 (over y).
Axes of the slice: x: 2, y: 2, z: 4, core: 2. Of those that a mesh axis runs over, the one named last changes fastest.
Arguments:
- queries: bfloat16 [32768, 4096], P('ctx', 'head'), may hold values from -8 to 8
- key_state_matrix: bfloat16 [32768, 1024], P('ctx', 'head'), may hold values from -4.5 to 4.5
- value_state_matrix: bfloat16 [32768, 1024], P('ctx', 'head'), may hold values from -6 to 6
- selected: int32 [64, 3], P('ctx'), may hold values from -1 to 59, as said below
- out_weight: bfloat16 [4096, 2048], P('head'), may hold values from -0.09375 to 0.09375
Outputs:
- mixed: bfloat16 [32768, 2048], P('ctx', 'head')
Inputs may be any that keep to these rules, and one draw needn't show every extreme that they name: `selected`: row j names blocks that lie on lower indices of ctx than block j (the block's index // 4 is the owning index), on three different indices; all rows of one index of ctx name at most one distinct block of each other index; a slot is -1 only when block j's index has fewer than three lower indices, and then exactly the missing slots are -1.
All inputs are finite; a program needn't handle non-finite values.
Results may differ from a plain program's by a relative error of at most 0.015.
Values may be sent and summed in bfloat16 or wider, within the bound.
A program may use at most 192 MiB of HBM per device.

v0:
```python
import jax
import jax.numpy as jnp
from jax import lax
from jax.sharding import PartitionSpec as P

HEAD_SIZE = 128
BLOCK_TOKENS = 512


def per_device(queries, key_state_matrix, value_state_matrix, selected, out_weight):
    ctx_count = lax.axis_size("ctx")
    ctx_index = lax.axis_index("ctx")
    tok_rows = queries.shape[0]
    blk_dev = tok_rows // BLOCK_TOKENS
    kv_width = key_state_matrix.shape[1]
    kv_heads = kv_width // HEAD_SIZE
    q_heads = queries.shape[1] // HEAD_SIZE
    query_group_size = q_heads // kv_heads
    request_count = blk_dev * 3
    wanted = selected.reshape(request_count)
    owners = wanted // blk_dev
    everyone = lax.all_gather(selected, "ctx", axis=0, tiled=True).reshape(ctx_count, request_count)
    asked = jnp.max(jnp.where(everyone // blk_dev == ctx_index, everyone, -1), axis=1)
    local_block = jnp.clip(asked - ctx_index * blk_dev, 0, blk_dev - 1)
    stacked = jnp.concatenate([key_state_matrix, value_state_matrix], axis=1).reshape(
        blk_dev, BLOCK_TOKENS, 2 * kv_width
    )
    outgoing = jnp.where(
        (asked >= 0)[:, None, None], stacked[local_block], jnp.zeros((), jnp.bfloat16)
    )
    arrived = lax.all_to_all(outgoing, "ctx", split_axis=0, concat_axis=0, tiled=True)
    source = jnp.clip(owners, 0, ctx_count - 1)
    chosen = arrived[source]
    fetched_keys = chosen[:, :, :kv_width]
    fetched_values = chosen[:, :, kv_width:]
    score_scale = HEAD_SIZE ** (-0.5)
    causal = jnp.arange(BLOCK_TOKENS)[:, None] >= jnp.arange(BLOCK_TOKENS)[None, :]
    own_keys = key_state_matrix.reshape(blk_dev, BLOCK_TOKENS, kv_width)
    own_values = value_state_matrix.reshape(blk_dev, BLOCK_TOKENS, kv_width)
    far_keys = fetched_keys.reshape(blk_dev, 3 * BLOCK_TOKENS, kv_width)
    far_values = fetched_values.reshape(blk_dev, 3 * BLOCK_TOKENS, kv_width)
    live_slots = selected >= 0
    blocked_queries = queries.reshape(blk_dev, BLOCK_TOKENS, q_heads * HEAD_SIZE)

    def one_block(inputs):
        query_here, near_key, near_value, remote_key, remote_value, live_here = inputs
        gathered_keys = jnp.concatenate([near_key, remote_key], axis=0).reshape(
            4 * BLOCK_TOKENS, kv_heads, HEAD_SIZE
        )
        gathered_values = jnp.concatenate([near_value, remote_value], axis=0).reshape(
            4 * BLOCK_TOKENS, kv_heads, HEAD_SIZE
        )
        live_sel = jnp.broadcast_to(
            jnp.repeat(live_here, BLOCK_TOKENS)[None, :], (BLOCK_TOKENS, 3 * BLOCK_TOKENS)
        )
        live = jnp.concatenate([causal, live_sel], axis=1)
        grouped = query_here.reshape(BLOCK_TOKENS, kv_heads, query_group_size, HEAD_SIZE)
        scores = (
            jnp.einsum("qhgd,khd->hgqk", grouped, gathered_keys, preferred_element_type=jnp.float32)
            * score_scale
        )
        scores = jnp.where(live[None, None], scores, -1e30)
        highest = jnp.max(scores, axis=-1, keepdims=True)
        expon = jnp.exp(scores - highest)
        weights = (expon / jnp.sum(expon, axis=-1, keepdims=True)).astype(jnp.bfloat16)
        output = jnp.einsum(
            "hgqk,khd->qhgd", weights, gathered_values, preferred_element_type=jnp.float32
        )
        return output.reshape(BLOCK_TOKENS, q_heads * HEAD_SIZE).astype(jnp.bfloat16)

    attended = lax.map(
        one_block, (blocked_queries, own_keys, own_values, far_keys, far_values, live_slots)
    )
    attended = attended.reshape(tok_rows, q_heads * HEAD_SIZE)
    partial_value = jnp.dot(attended, out_weight, preferred_element_type=jnp.float32)
    return lax.psum_scatter(partial_value, "head", scatter_dimension=1, tiled=True).astype(
        jnp.bfloat16
    )


def solution(mesh):
    return jax.shard_map(
        per_device,
        mesh=mesh,
        in_specs=(
            P("ctx", "head"),
            P("ctx", "head"),
            P("ctx", "head"),
            P("ctx", None),
            P("head", None),
        ),
        out_specs=P("ctx", "head"),
        check_vma=False,
    )
```

profile of v0, /device:TPU:0, one launch (start us, length us, event | category | flops | bytes accessed | tf_op | source)
XLA Modules:
  0.0 973.6 jit_solution(16265342644160364695)
XLA Ops:
  6.5 23.4 %all-gather = s32[16,4,3]{2,1,0:T(4,128)S(1)} all-gather(s32[1,4,3]{2,1,0:T(4,128)} %bitcast.96), channel_id=1, replica_groups=mesh['ctx'=16,'head'=2] {'ctx'}, dimensions={0}, use_global_device_ids=true | all-gather | bytes 816 | tf_op jit(solution)/shard_map/all_gather | solution.py:22
  30.3 4.8 pad_maximum_fusion
  35.1 9.3 gather_fusion
  44.4 14.0 %broadcast_select_fusion = bf16[16,512,1024]{2,1,0:T(8,128)(2,1)} fusion(bf16[16,512,1024]{2,1,0:T(8,128)(2,1)} %gather_fusion, pred[16]{0:T(512)(128)(4,1)S(1)} %broadcast_compare_fusion.1), kind=kLoop, calls=%fused_computation.34 | loop fusion | flops 8388608 | bytes 33554448 | tf_op jit(solution)/shard_map/jit(_where)/select_n | solution.py:28
  58.4 5.3 all-to-all-start
  63.8 296.5 %all-to-all-done = bf16[16,512,1024]{2,1,0:T(8,128)(2,1)} async-done(((bf16[16,512,1024]{2,1,0:T(8,128)(2,1)}), bf16[16,512,1024]{2,1,0:T(8,128)(2,1)}, u32[]{:S(2)}, u32[]{:S(2)}) %all-to-all-start) | async-done | bytes 16777248 | tf_op jit(solution)/shard_map/all_to_all | solution.py:31
  360.3 11.5 %gather_fusion.1 = bf16[12,512,1024]{2,1,0:T(8,128)(2,1)} fusion(bf16[16,512,1024]{2,1,0:T(8,128)(2,1)} %all-to-all-done, s32[1024]{0:T(1024)S(1)} %pad_clamp_fusion), kind=kCustom, calls=%fused_computation.1 | custom fusion | bytes 25165872 | tf_op jit(solution)/shard_map/gather | solution.py:33
  371.8 10.1 %fusion.28 = (bf16[12,512,512]{2,1,0:T(8,128)(2,1)}, bf16[12,512,512]{2,1,0:T(8,128)(2,1)}) fusion(bf16[12,512,1024]{2,1,0:T(8,128)(2,1)} %gather_fusion.1), kind=kLoop, calls=%fused_computation.58 | loop fusion | bytes 25165824 | tf_op jit(solution)/shard_map/slice | solution.py:34
  381.9 299.6 %while.11 = (s32[]{:T(128)}, bf16[4,512,2048]{2,1,0:T(8,128)(2,1)}, bf16[4,512,512]{2,1,0:T(8,128)(2,1)}, bf16[4,1536,512]{2,1,0:T(8,128)(2,1)}, pred[4,3]{1,0:T...) while((s32[]{:T(128)}, bf16[4,512,2048]{2,1,0:T(8,128)(2,1)}, ...), condition=%wide.region_5.6_spmd.clone, body=%wide.region_2.5_spmd.clone.sunk | while | flops 8701347840 | bytes 189344416 | solution.py:71
  381.9 3.2 constant_dynamic-slice_fusion.10
  385.2 0.7 copy.55
  385.9 1.6 copy.56
  387.5 1.3 constant_dynamic-slice_fusion.11
  388.9 1.0 copy.58
  389.9 1.7 constant_dynamic-slice_fusion.9
  391.7 2.5 copy.54
  394.4 0.6 pad_add_fusion.2
  395.0 32.1 %fusion.40 = (f32[4,4,512]{2,1,0:T(4,128)S(1)}, f32[4,4,512,2048]{2,3,1,0:T(8,128)}) fusion(pred[512,2048]{0,1:T(8,128)(4,1)S(1)} %pad_add_fusion.2, bf16[512,4,4,128]{0,3,2,1:T(8,128)(2,1)} %bitcast.85, bf16[1536,4,128]{2,0,1:T(8,128)(2,1)} %copy.56, bf16[512,4,128]{2,0,1:T(8,128)(2,1)} %copy.58), kind=kOutput, calls=%fused_computation.57.clone.1 | convolution fusion | flops 4366272512 | bytes 72384512 | tf_op jit(solution)/shard_map/while/body/eval_jaxpr/sub | solution.py:64
  427.1 1.6 copy.59
  428.9 23.5 %fusion.41 = bf16[4,128,4,512]{3,1,2,0:T(8,128)(2,1)} fusion(f32[4,4,512,2048]{2,3,1,0:T(8,128)} %get-tuple-element.176, f32[4,4,512]{2,1,0:T(4,128)S(1)} %get-tuple-element.177, bf16[1536,4,128]{0,2,1:T(8,128)(2,1)} %bitcast.88, bf16[512,4,128]{0,2,1:T(8,128)(2,1)S(1)} %bitcast.92), kind=kOutput, calls=%fused_computation.18.clone.1 | convolution fusion | flops 4333764608 | bytes 71335936 | tf_op jit(solution)/shard_map/while/body/eval_jaxpr/hgqk,khd->qhgd/dot_general | solution.py:66
  452.4 2.9 copy.61
  455.4 1.5 constant_dynamic-update-slice_fusion.2
  456.8 3.2 constant_dynamic-slice_fusion.10
  460.1 0.7 copy.55
  460.8 1.6 copy.56
  462.4 1.3 constant_dynamic-slice_fusion.11
  463.9 1.0 copy.58
  464.8 1.7 constant_dynamic-slice_fusion.9
  466.6 2.5 copy.54
  469.3 0.6 pad_add_fusion.2
  469.9 32.0 %fusion.40 = (f32[4,4,512]{2,1,0:T(4,128)S(1)}, f32[4,4,512,2048]{2,3,1,0:T(8,128)}) fusion(pred[512,2048]{0,1:T(8,128)(4,1)S(1)} %pad_add_fusion.2, bf16[512,4,4,128]{0,3,2,1:T(8,128)(2,1)} %bitcast.85, bf16[1536,4,128]{2,0,1:T(8,128)(2,1)} %copy.56, bf16[512,4,128]{2,0,1:T(8,128)(2,1)} %copy.58), kind=kOutput, calls=%fused_computation.57.clone.1 | convolution fusion | flops 4366272512 | bytes 72384512 | tf_op jit(solution)/shard_map/while/body/eval_jaxpr/sub | solution.py:64
  502.0 1.6 copy.59
  503.8 23.5 %fusion.41 = bf16[4,128,4,512]{3,1,2,0:T(8,128)(2,1)} fusion(f32[4,4,512,2048]{2,3,1,0:T(8,128)} %get-tuple-element.176, f32[4,4,512]{2,1,0:T(4,128)S(1)} %get-tuple-element.177, bf16[1536,4,128]{0,2,1:T(8,128)(2,1)} %bitcast.88, bf16[512,4,128]{0,2,1:T(8,128)(2,1)S(1)} %bitcast.92), kind=kOutput, calls=%fused_computation.18.clone.1 | convolution fusion | flops 4333764608 | bytes 71335936 | tf_op jit(solution)/shard_map/while/body/eval_jaxpr/hgqk,khd->qhgd/dot_general | solution.py:66
  527.3 2.9 copy.61
  530.2 1.5 constant_dynamic-update-slice_fusion.2
  531.7 3.2 constant_dynamic-slice_fusion.10
  535.0 0.7 copy.55
  535.7 1.6 copy.56
  537.3 1.3 constant_dynamic-slice_fusion.11
  538.7 1.0 copy.58
  539.7 1.7 constant_dynamic-slice_fusion.9
  541.5 2.5 copy.54
  544.2 0.6 pad_add_fusion.2
  544.8 32.1 %fusion.40 = (f32[4,4,512]{2,1,0:T(4,128)S(1)}, f32[4,4,512,2048]{2,3,1,0:T(8,128)}) fusion(pred[512,2048]{0,1:T(8,128)(4,1)S(1)} %pad_add_fusion.2, bf16[512,4,4,128]{0,3,2,1:T(8,128)(2,1)} %bitcast.85, bf16[1536,4,128]{2,0,1:T(8,128)(2,1)} %copy.56, bf16[512,4,128]{2,0,1:T(8,128)(2,1)} %copy.58), kind=kOutput, calls=%fused_computation.57.clone.1 | convolution fusion | flops 4366272512 | bytes 72384512 | tf_op jit(solution)/shard_map/while/body/eval_jaxpr/sub | solution.py:64
  576.9 1.6 copy.59
  578.7 23.5 %fusion.41 = bf16[4,128,4,512]{3,1,2,0:T(8,128)(2,1)} fusion(f32[4,4,512,2048]{2,3,1,0:T(8,128)} %get-tuple-element.176, f32[4,4,512]{2,1,0:T(4,128)S(1)} %get-tuple-element.177, bf16[1536,4,128]{0,2,1:T(8,128)(2,1)} %bitcast.88, bf16[512,4,128]{0,2,1:T(8,128)(2,1)S(1)} %bitcast.92), kind=kOutput, calls=%fused_computation.18.clone.1 | convolution fusion | flops 4333764608 | bytes 71335936 | tf_op jit(solution)/shard_map/while/body/eval_jaxpr/hgqk,khd->qhgd/dot_general | solution.py:66
  602.2 2.9 copy.61
  605.2 1.5 constant_dynamic-update-slice_fusion.2
  606.6 3.2 constant_dynamic-slice_fusion.10
  609.9 0.7 copy.55
  610.6 1.6 copy.56
  612.2 1.3 constant_dynamic-slice_fusion.11
  613.7 1.0 copy.58
  614.6 1.7 constant_dynamic-slice_fusion.9
  616.4 2.5 copy.54
  619.1 0.6 pad_add_fusion.2
  619.7 32.1 %fusion.40 = (f32[4,4,512]{2,1,0:T(4,128)S(1)}, f32[4,4,512,2048]{2,3,1,0:T(8,128)}) fusion(pred[512,2048]{0,1:T(8,128)(4,1)S(1)} %pad_add_fusion.2, bf16[512,4,4,128]{0,3,2,1:T(8,128)(2,1)} %bitcast.85, bf16[1536,4,128]{2,0,1:T(8,128)(2,1)} %copy.56, bf16[512,4,128]{2,0,1:T(8,128)(2,1)} %copy.58), kind=kOutput, calls=%fused_computation.57.clone.1 | convolution fusion | flops 4366272512 | bytes 72384512 | tf_op jit(solution)/shard_map/while/body/eval_jaxpr/sub | solution.py:64
  651.8 1.6 copy.59
  653.6 23.5 %fusion.41 = bf16[4,128,4,512]{3,1,2,0:T(8,128)(2,1)} fusion(f32[4,4,512,2048]{2,3,1,0:T(8,128)} %get-tuple-element.176, f32[4,4,512]{2,1,0:T(4,128)S(1)} %get-tuple-element.177, bf16[1536,4,128]{0,2,1:T(8,128)(2,1)} %bitcast.88, bf16[512,4,128]{0,2,1:T(8,128)(2,1)S(1)} %bitcast.92), kind=kOutput, calls=%fused_computation.18.clone.1 | convolution fusion | flops 4333764608 | bytes 71335936 | tf_op jit(solution)/shard_map/while/body/eval_jaxpr/hgqk,khd->qhgd/dot_general | solution.py:66
  677.1 2.9 copy.61
  680.1 1.4 constant_dynamic-update-slice_fusion.2
  681.5 24.1 %fusion.29 = f32[2048,2048]{1,0:T(8,128)} fusion(bf16[2048,2048]{1,0:T(8,128)(2,1)} %bitcast.97, bf16[2048,2048]{1,0:T(8,128)(2,1)} %param.11), kind=kOutput, calls=%fused_computation.59 | convolution fusion | flops 17179869184 | bytes 33554432 | tf_op jit(solution)/shard_map/dot_general | solution.py:75
  705.6 255.1 %reduce-scatter.2.cloned.1.call-done = f32[2048,1024]{1,0:T(8,128)} async-done(((f32[2048,2048]{1,0:T(8,128)}), f32[2048,1024]{1,0:T(8,128)}) %reduce-scatter.2.cloned.1.call-update) | async-done | bytes 8388624 | tf_op jit(solution)/shard_map/reduce_scatter | solution.py:76
  960.7 6.1 convert_element_type.22
  (51 shorter events, 3.0 us)
Async XLA Ops:
  58.4 5.3 copy-start.1
  58.4 302.0 %all-to-all-start = ((bf16[16,512,1024]{2,1,0:T(8,128)(2,1)}), bf16[16,512,1024]{2,1,0:T(8,128)(2,1)}, u32[]{:S(2)}, u32[]{:S(2)}) async-start(bf16[16,512,1024]{2,1,0:T(8,128)(2,1)} %broadcast_select_fusion), calls=%async_computation | async-start | bytes 33554432 | tf_op jit(solution)/shard_map/all_to_all | solution.py:31
  63.6 897.1 %reduce-scatter.2.cloned.1.call-start = ((), (), s32[]{:S(2)}) async-start(), calls=%async_computation.2 | async-start | bytes 25165824 | tf_op jit(solution)/shard_map/reduce_scatter | solution.py:76
  395.0 32.1 %copy-start = (bf16[1,1536,512]{2,1,0:T(8,128)(2,1)S(1)}, bf16[1,1536,512]{2,1,0:T(8,128)(2,1)}, u32[]{:S(2)}) copy-start(bf16[1,1536,512]{2,1,0:T(8,128)(2,1)} %get-tuple-element.178) | copy-start | bytes 4718596 | tf_op jit(solution)/shard_map/while
  469.9 32.1 %copy-start = (bf16[1,1536,512]{2,1,0:T(8,128)(2,1)S(1)}, bf16[1,1536,512]{2,1,0:T(8,128)(2,1)}, u32[]{:S(2)}) copy-start(bf16[1,1536,512]{2,1,0:T(8,128)(2,1)} %get-tuple-element.178) | copy-start | bytes 4718596 | tf_op jit(solution)/shard_map/while
  544.8 32.1 %copy-start = (bf16[1,1536,512]{2,1,0:T(8,128)(2,1)S(1)}, bf16[1,1536,512]{2,1,0:T(8,128)(2,1)}, u32[]{:S(2)}) copy-start(bf16[1,1536,512]{2,1,0:T(8,128)(2,1)} %get-tuple-element.178) | copy-start | bytes 4718596 | tf_op jit(solution)/shard_map/while
  619.7 32.1 %copy-start = (bf16[1,1536,512]{2,1,0:T(8,128)(2,1)S(1)}, bf16[1,1536,512]{2,1,0:T(8,128)(2,1)}, u32[]{:S(2)}) copy-start(bf16[1,1536,512]{2,1,0:T(8,128)(2,1)} %get-tuple-element.178) | copy-start | bytes 4718596 | tf_op jit(solution)/shard_map/while
Sparse Core Ops, SparseCore 0:
  705.8 254.8 reduce-scatter.1
where the time goes:
time: 975 us; the launch traced here: 974 us
  waiting for transfers between devices  552 us (57%)
  matrix products  246 us (25%)
  local copies, waits for them, and re-layouts  105 us (11%)
  other arithmetic  28 us (3%)
  blocking collectives  23.4 us (2%)
  between operations  13.5 us (1%)
    all_to_all x1, waiting for transfers between devices, per_device(): lax.all_to_all(outgoing, 'ctx', split_axis=0, concat_axis=0, tiled=True)  297 us
    reduce_scatter x1, waiting for transfers between devices, per_device(): lax.psum_scatter(partial_value, 'head', scatter_dimension=1, tiled=True)  255 us
    sub x4, matrix products, one_block(): expon = jnp.exp(scores - highest)  128 us
    dot_general x4, matrix products, one_block(): jnp.einsum('hgqk,khd->qhgd', weights, gathered_values, preferred_element_...  94.1 us
    dynamic_slice x32, local copies, waits for them, and re-layouts, per_device(): lax.map(one_block, (blocked_queries, own_keys, own_values, far_keys, far_...  45.8 us
    dot_general x1, matrix products, per_device(): jnp.dot(attended, out_weight, preferred_element_type=jnp.float32)  24.1 us
    all_gather x1, blocking collectives, per_device(): lax.all_gather(selected, 'ctx', axis=0, tiled=True)  23.4 us
  transfers between devices with their start and end apart: 2, of which 2 were waited for; matrix products, arithmetic and copies ran while one was open for 0% of the time, Pallas kernels for 0%

commit v1 on v0

v1 whole, which is shorter than its diff:
```python
import functools

import jax
import jax.numpy as jnp
from jax import lax
from jax.experimental import pallas as pl
from jax.experimental.pallas import tpu as pltpu
from jax.sharding import PartitionSpec as P

HEAD_SIZE = 128
BLOCK_TOKENS = 512
ROW_TILE = 256
EXPONENT_SCALE = HEAD_SIZE ** (-0.5) * 1.4426950408889634
NT = (((1,), (1,)), ((), ()))


def pack_kernel(block_ref, key_ref, value_ref, out_ref):
    out_ref[0, :, :HEAD_SIZE] = key_ref[...]
    out_ref[0, :, HEAD_SIZE:] = value_ref[...]


def pack_head(local_block, keys, values, head):
    count = local_block.shape[0]
    spec = pl.BlockSpec((BLOCK_TOKENS, HEAD_SIZE), lambda i, block: (block[i], head))
    return pl.pallas_call(
        pack_kernel,
        grid_spec=pltpu.PrefetchScalarGridSpec(
            num_scalar_prefetch=1,
            grid=(count,),
            in_specs=[spec, spec],
            out_specs=pl.BlockSpec((1, BLOCK_TOKENS, 2 * HEAD_SIZE), lambda i, block: (i, 0, 0)),
        ),
        out_shape=jax.ShapeDtypeStruct((count, BLOCK_TOKENS, 2 * HEAD_SIZE), jnp.bfloat16),
        cost_estimate=pl.CostEstimate(
            flops=0, bytes_accessed=count * BLOCK_TOKENS * 2 * HEAD_SIZE * 4, transcendentals=0
        ),
        name="pack_head",
    )(local_block, keys, values)


def attention_kernel(
    first, group, source_ref, live_ref, query_ref, key_ref, value_ref, far0, far1, far2, out_ref
):
    block = pl.program_id(0) + first
    far = (far0, far1, far2)
    offset = [jnp.where(live_ref[3 * block + j] > 0, 0.0, -1e30).astype(jnp.float32) for j in range(3)]
    ones = jnp.ones((BLOCK_TOKENS, HEAD_SIZE), jnp.bfloat16)
    row = lax.broadcasted_iota(jnp.int32, (ROW_TILE, ROW_TILE), 0)
    column = lax.broadcasted_iota(jnp.int32, (ROW_TILE, ROW_TILE), 1)
    causal = row >= column
    own_value = jnp.concatenate([value_ref[...], ones], axis=1)
    far_value = [jnp.concatenate([ref[0, :, HEAD_SIZE:], ones], axis=1) for ref in far]
    for tile in range(BLOCK_TOKENS // ROW_TILE):
        rows = slice(tile * ROW_TILE, (tile + 1) * ROW_TILE)
        for member in range(group):
            columns = slice(member * HEAD_SIZE, (member + 1) * HEAD_SIZE)
            query = query_ref[rows, columns]
            scores = []
            diagonal = lax.dot_general(
                query, key_ref[rows, :], NT, preferred_element_type=jnp.float32
            )
            diagonal = jnp.where(causal, diagonal, -1e30)
            highest = jnp.max(diagonal, axis=1, keepdims=True)
            scores.append((diagonal, own_value[rows], None))
            if tile > 0:
                before = lax.dot_general(
                    query, key_ref[: tile * ROW_TILE, :], NT, preferred_element_type=jnp.float32
                )
                highest = jnp.maximum(highest, jnp.max(before, axis=1, keepdims=True))
                scores.append((before, own_value[: tile * ROW_TILE], None))
            for j in range(3):
                remote = lax.dot_general(
                    query, far[j][0, :, :HEAD_SIZE], NT, preferred_element_type=jnp.float32
                )
                highest = jnp.maximum(
                    highest, jnp.max(remote, axis=1, keepdims=True) + offset[j]
                )
                scores.append((remote, far_value[j], offset[j]))
            highest = highest * EXPONENT_SCALE
            total = None
            for score, value, shift in scores:
                base = highest if shift is None else highest - shift
                weight = jnp.exp2(score * EXPONENT_SCALE - base).astype(jnp.bfloat16)
                term = jnp.dot(weight, value, preferred_element_type=jnp.float32)
                total = term if total is None else total + term
            out_ref[rows, columns] = (total[:, :HEAD_SIZE] / total[:, HEAD_SIZE:]).astype(
                jnp.bfloat16
            )


def attend_head(source, live, queries, keys, values, arrived, head, group, first, blocks):
    width = group * HEAD_SIZE

    def own(i, source, live):
        return (i + first, head)

    def slot(j):
        return pl.BlockSpec(
            (1, BLOCK_TOKENS, 2 * HEAD_SIZE),
            lambda i, source, live: (source[3 * (i + first) + j], 0, 0),
        )

    pairs = blocks * group * BLOCK_TOKENS * 4 * BLOCK_TOKENS
    return pl.pallas_call(
        functools.partial(attention_kernel, first, group),
        grid_spec=pltpu.PrefetchScalarGridSpec(
            num_scalar_prefetch=2,
            grid=(blocks,),
            in_specs=[
                pl.BlockSpec((BLOCK_TOKENS, width), own),
                pl.BlockSpec((BLOCK_TOKENS, HEAD_SIZE), own),
                pl.BlockSpec((BLOCK_TOKENS, HEAD_SIZE), own),
                slot(0),
                slot(1),
                slot(2),
            ],
            out_specs=pl.BlockSpec((BLOCK_TOKENS, width), lambda i, source, live: (i, 0)),
        ),
        out_shape=jax.ShapeDtypeStruct((blocks * BLOCK_TOKENS, width), jnp.bfloat16),
        compiler_params=pltpu.CompilerParams(vmem_limit_bytes=40 * 1024 * 1024),
        cost_estimate=pl.CostEstimate(
            flops=pairs * HEAD_SIZE * 8,
            bytes_accessed=blocks * BLOCK_TOKENS * 2 * (2 * width + 8 * HEAD_SIZE),
            transcendentals=pairs,
        ),
        name="attend_head",
    )(source, live, queries, keys, values, arrived, arrived, arrived)


def per_device(queries, keys, values, selected, out_weight):
    ctx_count = lax.axis_size("ctx")
    ctx_index = lax.axis_index("ctx")
    head_count = lax.axis_size("head")
    head_index = lax.axis_index("head")
    blk_dev = queries.shape[0] // BLOCK_TOKENS
    kv_heads = keys.shape[1] // HEAD_SIZE
    group = queries.shape[1] // HEAD_SIZE // kv_heads
    width = group * HEAD_SIZE
    out_columns = out_weight.shape[1] // head_count
    request_count = blk_dev * 3

    turns = [[(i, (i + s) % head_count) for i in range(head_count)] for s in range(head_count)]
    weights = []
    for s in range(head_count):
        start = lax.rem(head_index + s, head_count) * out_columns
        share = lax.dynamic_slice_in_dim(out_weight, start, out_columns, axis=1)
        weights.append(share if s == 0 else lax.ppermute(share, "head", turns[s]))

    wanted = selected.reshape(request_count)
    everyone = lax.all_gather(selected, "ctx", axis=0, tiled=True).reshape(ctx_count, request_count)
    asked = jnp.max(jnp.where(everyone // blk_dev == ctx_index, everyone, -1), axis=1)
    local_block = jnp.clip(asked - ctx_index * blk_dev, 0, blk_dev - 1).astype(jnp.int32)
    source = jnp.clip(wanted // blk_dev, 0, ctx_count - 1).astype(jnp.int32)
    live = (wanted >= 0).astype(jnp.int32)

    arrived = []
    for head in range(kv_heads):
        outgoing = pack_head(local_block, keys, values, head)
        arrived.append(
            lax.all_to_all(outgoing, "ctx", split_axis=0, concat_axis=0, tiled=True)
        )

    def project(parts, head):
        total = None
        rows = slice(head * width, (head + 1) * width)
        for part, weight in zip(parts, weights):
            term = jnp.dot(part, weight[rows], preferred_element_type=jnp.float32)
            total = term if total is None else total + term
        return total

    def spread(attended):
        return [attended] + [lax.ppermute(attended, "head", turns[s]) for s in range(1, head_count)]

    total = None
    for head in range(kv_heads - 1):
        attended = attend_head(
            source, live, queries, keys, values, arrived[head], head, group, 0, blk_dev
        )
        term = project(spread(attended), head)
        total = term if total is None else total + term
    head = kv_heads - 1
    half = blk_dev // 2
    outputs = []
    for first, blocks in ((0, half), (half, blk_dev - half)):
        attended = attend_head(
            source, live, queries, keys, values, arrived[head], head, group, first, blocks
        )
        term = project(spread(attended), head)
        rows = slice(first * BLOCK_TOKENS, (first + blocks) * BLOCK_TOKENS)
        outputs.append((term if total is None else total[rows] + term).astype(jnp.bfloat16))
    return jnp.concatenate(outputs, axis=0)


def solution(mesh):
    return jax.shard_map(
        per_device,
        mesh=mesh,
        in_specs=(
            P("ctx", "head"),
            P("ctx", "head"),
            P("ctx", "head"),
            P("ctx", None),
            P("head", None),
        ),
        out_specs=P("ctx", "head"),
        check_vma=False,
    )
```

time: 975 us -> 626 us (0.64); the launches traced: 974 us -> 615 us
  waiting for transfers between devices: 552 us -> 289 us
  matrix products: 246 us -> 73.5 us
  Pallas kernels: 0 us -> 147 us
  local copies, waits for them, and re-layouts: 105 us -> 8.16 us
  starting transfers between devices: 5.33 us -> 69.7 us
  other arithmetic: 28 us -> 3.3 us
  between operations: 13.5 us -> 0.38 us
    reduce_scatter x1 -> x0, waiting for transfers between devices: 255 us -> none  [per_device(): lax.psum_scatter(partial_value, 'head', scatter_dimension=1, tiled=True)]
    pallas_call x0 -> x9, Pallas kernels: none -> 147 us  [the longest x5 103 us: attend_head(): pl.pallas_call(functools.partial(attention_kernel, first, group), grid_sp...]
    sub x4 -> x0, matrix products: 128 us -> none  [one_block(): expon = jnp.exp(scores - highest)]
    all_to_all x1 -> x4, waiting for transfers between devices: 297 us -> 200 us  [per_device(): lax.all_to_all(outgoing, 'ctx', split_axis=0, concat_axis=0, tiled=True)]
    ppermute x0 -> x6, waiting for transfers between devices: none -> 89.4 us  [the longest x5 89.4 us: spread(): lax.ppermute(attended, 'head', turns[s])]
    all_to_all x1 -> x4, starting transfers between devices: 5.29 us -> 63.6 us  [per_device(): lax.all_to_all(outgoing, 'ctx', split_axis=0, concat_axis=0, tiled=True)]
    dot_general x5 -> x10, matrix products: 118 us -> 73.5 us  [project(): term = jnp.dot(part, weight[rows], preferred_element_type=jnp.float32)]
    dynamic_slice x32 -> x1, local copies, waits for them, and re-layouts: 45.8 us -> 4.79 us  [per_device(): share = lax.dynamic_slice_in_dim(out_weight, start, out_columns, axis=1)]
  transfers between devices with their start and end apart: 2 -> 10, of which waited for: 2 -> 7; matrix products, arithmetic and copies ran while one was open for 0% -> 12% of each run, Pallas kernels for 0% -> 22%
where the time goes in v1:
time: 626 us; the launch traced here: 615 us
  waiting for transfers between devices  289 us (46%)
  Pallas kernels  147 us (23%)
  matrix products  73.5 us (12%)
  starting transfers between devices  69.7 us (11%)
  blocking collectives  23.4 us (4%)
  local copies, waits for them, and re-layouts  8.16 us (1%)
    all_to_all x4, waiting for transfers between devices, per_device(): lax.all_to_all(outgoing, 'ctx', split_axis=0, concat_axis=0, tiled=True)  200 us
    pallas_call x5, Pallas kernels, attend_head(): pl.pallas_call(functools.partial(attention_kernel, first, group), grid_sp...  103 us
    ppermute x5, waiting for transfers between devices, spread(): lax.ppermute(attended, 'head', turns[s])  89.4 us
    dot_general x10, matrix products, project(): term = jnp.dot(part, weight[rows], preferred_element_type=jnp.float32)  73.5 us
    all_to_all x4, starting transfers between devices, per_device(): lax.all_to_all(outgoing, 'ctx', split_axis=0, concat_axis=0, tiled=True)  63.6 us
    pallas_call x4, Pallas kernels, pack_head(): pl.pallas_call(pack_kernel, grid_spec=pltpu.PrefetchScalarGridSpec(num_sc...  44 us
    all_gather x1, blocking collectives, per_device(): lax.all_gather(selected, 'ctx', axis=0, tiled=True)  23.4 us
  transfers between devices with their start and end apart: 10, of which 7 were waited for; matrix products, arithmetic and copies ran while one was open for 12% of the time, Pallas kernels for 22%

profile of v1, /device:TPU:0, one launch (start us, length us, event | category | flops | bytes accessed | tf_op | source)
XLA Modules:
  0.0 614.6 jit_solution(14452554920755335483)
XLA Ops:
  0.0 23.4 %all-gather = s32[16,4,3]{2,1,0:T(4,128)S(1)} all-gather(s32[1,4,3]{2,1,0:T(4,128)} %bitcast.15), channel_id=1, replica_groups=mesh['ctx'=16,'head'=2] {'ctx'}, dimensions={0}, use_global_device_ids=true | all-gather | bytes 816 | tf_op jit(solution)/shard_map/all_gather | solution.py:150
  23.4 0.1 select_reduce_fusion
  23.5 0.1 reduce_max.14
  23.6 0.1 reduce_max.18
  23.7 0.6 subtract_clamp_fusion.block_ref
  24.3 11.0 %pack_head.5 = bf16[16,512,256]{2,1,0:T(8,128)(2,1)} custom-call(s32[16]{0:T(128)} %subtract_clamp_fusion.block_ref, bf16[2048,512]{1,0:T(8,128)(2,1)} %key_ref.17, bf16[2048,512]{1,0:T(8,128)(2,1)} %value_ref.17), custom_call_target="tpu_custom_call" | custom-call | bytes 8388608 | tf_op jit(solution)/shard_map/pack_head/pallas_call | solution.py:25
  35.3 4.5 all-to-all-start.1
  39.8 11.0 %pack_head.4 = bf16[16,512,256]{2,1,0:T(8,128)(2,1)} custom-call(s32[16]{0:T(128)} %subtract_clamp_fusion.block_ref, bf16[2048,512]{1,0:T(8,128)(2,1)} %key_ref.17, bf16[2048,512]{1,0:T(8,128)(2,1)} %value_ref.17), custom_call_target="tpu_custom_call" | custom-call | bytes 8388608 | tf_op jit(solution)/shard_map/pack_head/pallas_call | solution.py:25
  50.8 66.6 %all-to-all-done.1.far0.far1.far2 = bf16[16,512,256]{2,1,0:T(8,128)(2,1)} async-done(((bf16[16,512,256]{2,1,0:T(8,128)(2,1)}), bf16[16,512,256]{2,1,0:T(8,128)(2,1)}, u32[]{:S(2)}, u32[]{:S(2)}) %all-to-all-start.1) | async-done | bytes 4194336 | tf_op jit(solution)/shard_map/all_to_all | solution.py:160
  117.4 19.7 %all-to-all-start = ((bf16[16,512,256]{2,1,0:T(8,128)(2,1)}), bf16[16,512,256]{2,1,0:T(8,128)(2,1)}, u32[]{:S(2)}, u32[]{:S(2)}) async-start(bf16[16,512,256]{2,1,0:T(8,128)(2,1)} %pack_head.4), calls=%async_computation | async-start | bytes 8388608 | tf_op jit(solution)/shard_map/all_to_all | solution.py:160
  137.1 11.0 %pack_head.6 = bf16[16,512,256]{2,1,0:T(8,128)(2,1)} custom-call(s32[16]{0:T(128)} %subtract_clamp_fusion.block_ref, bf16[2048,512]{1,0:T(8,128)(2,1)} %key_ref.17, bf16[2048,512]{1,0:T(8,128)(2,1)} %value_ref.17), custom_call_target="tpu_custom_call" | custom-call | bytes 8388608 | tf_op jit(solution)/shard_map/pack_head/pallas_call | solution.py:25
  148.1 66.7 %all-to-all-done.far0.far1.far2 = bf16[16,512,256]{2,1,0:T(8,128)(2,1)} async-done(((bf16[16,512,256]{2,1,0:T(8,128)(2,1)}), bf16[16,512,256]{2,1,0:T(8,128)(2,1)}, u32[]{:S(2)}, u32[]{:S(2)}) %all-to-all-start) | async-done | bytes 4194336 | tf_op jit(solution)/shard_map/all_to_all | solution.py:160
  214.8 19.7 %all-to-all-start.2 = ((bf16[16,512,256]{2,1,0:T(8,128)(2,1)}), bf16[16,512,256]{2,1,0:T(8,128)(2,1)}, u32[]{:S(2)}, u32[]{:S(2)}) async-start(bf16[16,512,256]{2,1,0:T(8,128)(2,1)} %pack_head.6), calls=%async_computation.2 | async-start | bytes 8388608 | tf_op jit(solution)/shard_map/all_to_all | solution.py:160
  234.5 11.0 %pack_head.7 = bf16[16,512,256]{2,1,0:T(8,128)(2,1)} custom-call(s32[16]{0:T(128)} %subtract_clamp_fusion.block_ref, bf16[2048,512]{1,0:T(8,128)(2,1)} %key_ref.17, bf16[2048,512]{1,0:T(8,128)(2,1)} %value_ref.17), custom_call_target="tpu_custom_call" | custom-call | bytes 8388608 | tf_op jit(solution)/shard_map/pack_head/pallas_call | solution.py:25
  245.5 66.7 %all-to-all-done.2.far0.far1.far2 = bf16[16,512,256]{2,1,0:T(8,128)(2,1)} async-done(((bf16[16,512,256]{2,1,0:T(8,128)(2,1)}), bf16[16,512,256]{2,1,0:T(8,128)(2,1)}, u32[]{:S(2)}, u32[]{:S(2)}) %all-to-all-start.2) | async-done | bytes 4194336 | tf_op jit(solution)/shard_map/all_to_all | solution.py:160
  312.1 19.7 %all-to-all-start.3 = ((bf16[16,512,256]{2,1,0:T(8,128)(2,1)}), bf16[16,512,256]{2,1,0:T(8,128)(2,1)}, u32[]{:S(2)}, u32[]{:S(2)}) async-start(bf16[16,512,256]{2,1,0:T(8,128)(2,1)} %pack_head.7), calls=%async_computation.3 | async-start | bytes 8388608 | tf_op jit(solution)/shard_map/all_to_all | solution.py:160
  331.8 0.0 copy-start.5
  331.9 0.0 copy-start
  331.9 4.8 constant_dynamic-slice_fusion
  336.7 1.5 collective-permute-start.1
  338.2 0.0 copy-done.5
  338.2 0.1 reshape.5
  338.3 0.0 copy-done
  338.3 0.0 copy-start.1
  338.3 1.6 copy-done.1
  339.9 25.1 %attend_head.6 = bf16[2048,512]{1,0:T(8,128)(2,1)} custom-call(s32[12]{0:T(128)S(1)} %fusion.22.source_ref, s32[12]{0:T(128)S(1)} %compare_convert_fusion.live_ref, bf16[2048,2048]{1,0:T(8,128)(2,1)} %query_ref.9, bf16[2048,512]{1,0:T(8,128)(2,1)S(1)} %copy-done, bf16[2048,512]{1,0:T(8,128)(2,1)S(1)} %copy-done.1, ...), custom_call_target="tpu_custom_call" | custom-call | flops 17179869184 | bytes 8388608 | tf_op jit(solution)/shard_map/attend_head/pallas_call | solution.py:104
  365.0 0.5 collective-permute-start.2
  365.5 25.1 %attend_head.5 = bf16[2048,512]{1,0:T(8,128)(2,1)} custom-call(s32[12]{0:T(128)S(1)} %fusion.22.source_ref, s32[12]{0:T(128)S(1)} %compare_convert_fusion.live_ref, bf16[2048,2048]{1,0:T(8,128)(2,1)} %query_ref.9, bf16[2048,512]{1,0:T(8,128)(2,1)S(1)} %copy-done, bf16[2048,512]{1,0:T(8,128)(2,1)S(1)} %copy-done.1, ...), custom_call_target="tpu_custom_call" | custom-call | flops 17179869184 | bytes 8388608 | tf_op jit(solution)/shard_map/attend_head/pallas_call | solution.py:104
  390.6 1.5 collective-permute-start
  392.1 25.5 %attend_head.7 = bf16[2048,512]{1,0:T(8,128)(2,1)} custom-call(s32[12]{0:T(128)S(1)} %fusion.22.source_ref, s32[12]{0:T(128)S(1)} %compare_convert_fusion.live_ref, bf16[2048,2048]{1,0:T(8,128)(2,1)} %query_ref.9, bf16[2048,512]{1,0:T(8,128)(2,1)S(1)} %copy-done, bf16[2048,512]{1,0:T(8,128)(2,1)S(1)} %copy-done.1, ...), custom_call_target="tpu_custom_call" | custom-call | flops 17179869184 | bytes 8388608 | tf_op jit(solution)/shard_map/attend_head/pallas_call | solution.py:104
  417.6 0.5 collective-permute-start.3
  418.1 0.0 all-to-all-done.3.far0.far1.far2
  418.1 0.0 copy-start.2
  418.1 1.6 copy-done.2
  419.7 0.0 slice-start
  419.7 14.0 %attend_head.8 = bf16[1024,512]{1,0:T(8,128)(2,1)} custom-call(s32[12]{0:T(128)S(1)} %fusion.22.source_ref, s32[12]{0:T(128)S(1)} %compare_convert_fusion.live_ref, bf16[2048,2048]{1,0:T(8,128)(2,1)} %query_ref.9, bf16[2048,512]{1,0:T(8,128)(2,1)S(1)} %copy-done, bf16[2048,512]{1,0:T(8,128)(2,1)S(1)} %copy-done.2, ...), custom_call_target="tpu_custom_call" | custom-call | flops 8589934592 | bytes 4194304 | tf_op jit(solution)/shard_map/attend_head/pallas_call | solution.py:104
  433.7 0.0 slice-start.1
  433.7 1.5 collective-permute-start.4
  435.2 13.3 %attend_head.9 = bf16[1024,512]{1,0:T(8,128)(2,1)S(1)} custom-call(s32[12]{0:T(128)S(1)} %fusion.22.source_ref, s32[12]{0:T(128)S(1)} %compare_convert_fusion.live_ref, bf16[2048,2048]{1,0:T(8,128)(2,1)} %query_ref.9, bf16[2048,512]{1,0:T(8,128)(2,1)S(1)} %copy-done, bf16[2048,512]{1,0:T(8,128)(2,1)S(1)} %copy-done.2, ...), custom_call_target="tpu_custom_call" | custom-call | flops 8589934592 | bytes 4194304 | tf_op jit(solution)/shard_map/attend_head/pallas_call | solution.py:104
  448.5 0.0 slice-done
  448.5 0.0 slice-done.1
  448.5 7.2 %fusion.11 = f32[2048,1024]{1,0:T(8,128)} fusion(bf16[2048,512]{1,0:T(8,128)(2,1)} %attend_head.5, bf16[2048,2048]{1,0:T(8,128)(2,1)S(1)} %bitcast.13, s32[]{:T(128)S(6)} %select_n.25), kind=kOutput, calls=%fused_computation.15 | convolution fusion | flops 2147483648 | bytes 11534340 | tf_op jit(solution)/shard_map/dot_general | solution.py:167
  455.7 4.5 fusion.17
  460.2 3.2 fusion.15
  463.4 7.2 %fusion.7 = f32[2048,1024]{1,0:T(8,128)} fusion(bf16[2048,512]{1,0:T(8,128)(2,1)} %attend_head.6, bf16[2048,2048]{1,0:T(8,128)(2,1)S(1)} %bitcast.13, s32[]{:T(128)S(6)} %add.51, s32[]{:T(128)S(6)} %select_n.25), kind=kOutput, calls=%fused_computation.11 | convolution fusion | flops 2147483648 | bytes 11534344 | tf_op jit(solution)/shard_map/dot_general | solution.py:167
  470.6 7.2 %fusion.3 = f32[2048,1024]{1,0:T(8,128)} fusion(bf16[2048,512]{1,0:T(8,128)(2,1)} %attend_head.7, bf16[2048,2048]{1,0:T(8,128)(2,1)S(1)} %bitcast.13, s32[]{:T(128)S(6)} %add.52, s32[]{:T(128)S(6)} %select_n.25), kind=kOutput, calls=%fused_computation.7 | convolution fusion | flops 2147483648 | bytes 11534344 | tf_op jit(solution)/shard_map/dot_general | solution.py:167
  477.8 0.0 collective-permute-done.1
  477.8 0.5 collective-permute-start.5
  478.3 0.0 collective-permute-done.2
  478.3 7.4 %fusion.5 = f32[2048,1024]{1,0:T(8,128)} fusion(bf16[2048,512]{1,0:T(8,128)(2,1)} %collective-permute-done.2, bf16[2048,1024]{1,0:T(8,128)(2,1)} %collective-permute-done.1), kind=kOutput, calls=%fused_computation.9 | convolution fusion | flops 2147483648 | bytes 11534336 | tf_op jit(solution)/shard_map/dot_general | solution.py:167
  485.7 34.5 %collective-permute-done = bf16[2048,512]{1,0:T(8,128)(2,1)} collective-permute-done((bf16[2048,512]{1,0:T(8,128)(2,1)}, bf16[2048,512]{1,0:T(8,128)(2,1)}, u32[]{:S(2)}, u32[]{:S(2)}) %collective-permute-start) | collective-permute-done | bytes 2097184 | tf_op jit(solution)/shard_map/ppermute | solution.py:172
  520.3 7.6 %fusion.9 = f32[2048,1024]{1,0:T(8,128)} fusion(bf16[2048,512]{1,0:T(8,128)(2,1)} %collective-permute-done, bf16[2048,1024]{1,0:T(8,128)(2,1)} %collective-permute-done.1), kind=kOutput, calls=%fused_computation.13 | convolution fusion | flops 2147483648 | bytes 11534336 | tf_op jit(solution)/shard_map/dot_general | solution.py:167
  527.9 37.3 %collective-permute-done.3 = bf16[2048,512]{1,0:T(8,128)(2,1)} collective-permute-done((bf16[2048,512]{1,0:T(8,128)(2,1)}, bf16[2048,512]{1,0:T(8,128)(2,1)}, u32[]{:S(2)}, u32[]{:S(2)}) %collective-permute-start.3) | collective-permute-done | bytes 2097184 | tf_op jit(solution)/shard_map/ppermute | solution.py:172
  565.2 20.6 %add_add_fusion = f32[2048,1024]{1,0:T(8,128)} fusion(f32[2048,1024]{1,0:T(8,128)} %fusion.3, f32[2048,1024]{1,0:T(8,128)} %fusion.7, f32[2048,1024]{1,0:T(8,128)} %fusion.5, f32[2048,1024]{1,0:T(8,128)} %fusion.11, f32[2048,1024]{1,0:T(8,128)} %fusion.9, bf16[2048,512]{1,0:T(8,128)(2,1)} %collective-permute-done.3, bf16[2048,1024]{1,0:T(8,128)(2,1)} %collective-permute-done.1), kind=kOutput, calls=%fused_computation | convolution fusion | flops 2157969408 | bytes 53477376 | tf_op jit(solution)/shard_map/dot_general | solution.py:167
  585.8 0.0 copy-start.3
  585.8 0.0 copy-start.4
  585.8 1.8 collective-permute-done.4
  587.7 6.0 fusion.1
  593.7 15.8 %collective-permute-done.5 = bf16[1024,512]{1,0:T(8,128)(2,1)S(1)} collective-permute-done((bf16[1024,512]{1,0:T(8,128)(2,1)S(1)}, bf16[1024,512]{1,0:T(8,128)(2,1)S(1)}, u32[]{:S(2)}, u32[]{:S(2)}) %collective-permute-start.5) | collective-permute-done | bytes 1048608 | tf_op jit(solution)/shard_map/ppermute | solution.py:172
  609.5 0.0 copy-done.3
  609.5 0.0 copy-done.4
  609.5 2.5 fusion
  612.0 2.5 pad_maximum_fusion
  (3 shorter events, 0.0 us)
Async XLA Ops:
  35.3 82.2 %all-to-all-start.1 = ((bf16[16,512,256]{2,1,0:T(8,128)(2,1)}), bf16[16,512,256]{2,1,0:T(8,128)(2,1)}, u32[]{:S(2)}, u32[]{:S(2)}) async-start(bf16[16,512,256]{2,1,0:T(8,128)(2,1)} %pack_head.5), calls=%async_computation.1 | async-start | bytes 8388608 | tf_op jit(solution)/shard_map/all_to_all | solution.py:160
  117.4 97.4 %all-to-all-start = ((bf16[16,512,256]{2,1,0:T(8,128)(2,1)}), bf16[16,512,256]{2,1,0:T(8,128)(2,1)}, u32[]{:S(2)}, u32[]{:S(2)}) async-start(bf16[16,512,256]{2,1,0:T(8,128)(2,1)} %pack_head.4), calls=%async_computation | async-start | bytes 8388608 | tf_op jit(solution)/shard_map/all_to_all | solution.py:160
  214.8 97.4 %all-to-all-start.2 = ((bf16[16,512,256]{2,1,0:T(8,128)(2,1)}), bf16[16,512,256]{2,1,0:T(8,128)(2,1)}, u32[]{:S(2)}, u32[]{:S(2)}) async-start(bf16[16,512,256]{2,1,0:T(8,128)(2,1)} %pack_head.6), calls=%async_computation.2 | async-start | bytes 8388608 | tf_op jit(solution)/shard_map/all_to_all | solution.py:160
  312.1 106.0 %all-to-all-start.3 = ((bf16[16,512,256]{2,1,0:T(8,128)(2,1)}), bf16[16,512,256]{2,1,0:T(8,128)(2,1)}, u32[]{:S(2)}, u32[]{:S(2)}) async-start(bf16[16,512,256]{2,1,0:T(8,128)(2,1)} %pack_head.7), calls=%async_computation.3 | async-start | bytes 8388608 | tf_op jit(solution)/shard_map/all_to_all | solution.py:160
  331.8 6.3 %copy-start.5 = (s32[4,3]{1,0:T(4,128)S(1)}, s32[4,3]{1,0:T(4,128)}, u32[]{:S(2)}) copy-start(s32[4,3]{1,0:T(4,128)} %param.8) | copy-start | bytes 148
  331.9 6.4 %copy-start = (bf16[2048,512]{1,0:T(8,128)(2,1)S(1)}, bf16[2048,512]{1,0:T(8,128)(2,1)}, u32[]{:S(2)}) copy-start(bf16[2048,512]{1,0:T(8,128)(2,1)} %key_ref.17) | copy-start | bytes 6291460
  336.7 141.1 %collective-permute-start.1 = (bf16[2048,1024]{1,0:T(8,128)(2,1)}, bf16[2048,1024]{1,0:T(8,128)(2,1)}, u32[]{:S(2)}, u32[]{:S(2)}) collective-permute-start(bf16[2048,1024]{1,0:T(8,128)(2,1)} %constant_dynamic-slice_fusion), channel_id=1, source_target_pairs={{0,1},{1,0},{2,3},{3,2},{4,5},{5,4},{6,7},{7,6},{8,9},{9,8},{10,11... | collective-permute-start | bytes 12582920 | tf_op jit(solution)/shard_map/ppermute | solution.py:147
  338.3 1.6 copy-start.1
  365.0 113.3 %collective-permute-start.2 = (bf16[2048,512]{1,0:T(8,128)(2,1)}, bf16[2048,512]{1,0:T(8,128)(2,1)}, u32[]{:S(2)}, u32[]{:S(2)}) collective-permute-start(bf16[2048,512]{1,0:T(8,128)(2,1)} %attend_head.6), channel_id=1, source_target_pairs={{0,1},{1,0},{2,3},{3,2},{4,5},{5,4},{6,7},{7,6},{8,9},{9,8},{10,11... | collective-permute-start | bytes 6291464 | tf_op jit(solution)/shard_map/ppermute | solution.py:172
  390.6 129.7 %collective-permute-start = (bf16[2048,512]{1,0:T(8,128)(2,1)}, bf16[2048,512]{1,0:T(8,128)(2,1)}, u32[]{:S(2)}, u32[]{:S(2)}) collective-permute-start(bf16[2048,512]{1,0:T(8,128)(2,1)} %attend_head.5), channel_id=1, source_target_pairs={{0,1},{1,0},{2,3},{3,2},{4,5},{5,4},{6,7},{7,6},{8,9},{9,8},{10,11... | collective-permute-start | bytes 6291464 | tf_op jit(solution)/shard_map/ppermute | solution.py:172
  417.6 147.6 %collective-permute-start.3 = (bf16[2048,512]{1,0:T(8,128)(2,1)}, bf16[2048,512]{1,0:T(8,128)(2,1)}, u32[]{:S(2)}, u32[]{:S(2)}) collective-permute-start(bf16[2048,512]{1,0:T(8,128)(2,1)} %attend_head.7), channel_id=1, source_target_pairs={{0,1},{1,0},{2,3},{3,2},{4,5},{5,4},{6,7},{7,6},{8,9},{9,8},{10,11... | collective-permute-start | bytes 6291464 | tf_op jit(solution)/shard_map/ppermute | solution.py:172
  418.1 1.6 copy-start.2
  419.7 28.8 %slice-start = ((s8[8388608]{0:T(1024)(128)(4,1)}), s8[4194304]{0:T(1024)(128)(4,1)S(1)}, s32[]{:S(2)}) async-start(s8[8388608]{0:T(1024)(128)(4,1)} %bitcast.12), calls=%async_computation.4 | async-start | bytes 8388608
  433.7 14.8 %slice-start.1 = ((s8[8388608]{0:T(1024)(128)(4,1)}), s8[4194304]{0:T(1024)(128)(4,1)S(1)}, s32[]{:S(2)}) async-start(s8[8388608]{0:T(1024)(128)(4,1)} %bitcast.12), calls=%async_computation.5 | async-start | bytes 8388608
  433.7 154.0 %collective-permute-start.4 = (bf16[1024,512]{1,0:T(8,128)(2,1)}, bf16[1024,512]{1,0:T(8,128)(2,1)}, u32[]{:S(2)}, u32[]{:S(2)}) collective-permute-start(bf16[1024,512]{1,0:T(8,128)(2,1)} %attend_head.8), channel_id=1, source_target_pairs={{0,1},{1,0},{2,3},{3,2},{4,5},{5,4},{6,7},{7,6},{8,9},{9,8},{10,11... | collective-permute-start | bytes 3145736 | tf_op jit(solution)/shard_map/ppermute | solution.py:172
  477.8 131.7 %collective-permute-start.5 = (bf16[1024,512]{1,0:T(8,128)(2,1)S(1)}, bf16[1024,512]{1,0:T(8,128)(2,1)S(1)}, u32[]{:S(2)}, u32[]{:S(2)}) collective-permute-start(bf16[1024,512]{1,0:T(8,128)(2,1)S(1)} %attend_head.9), channel_id=1, source_target_pairs={{0,1},{1,0},{2,3},{3,2},{4,5},{5,4},{6,7},{7,6},{8,9},{9,8},{10,11... | collective-permute-start | bytes 3145736 | tf_op jit(solution)/shard_map/ppermute | solution.py:172
  585.8 23.6 %copy-start.3 = (f32[2048,1024]{1,0:T(8,128)S(1)}, f32[2048,1024]{1,0:T(8,128)}, u32[]{:S(2)}) copy-start(f32[2048,1024]{1,0:T(8,128)} %add_add_fusion) | copy-start | bytes 25165828
  585.8 23.6 %copy-start.4 = (f32[1024,1024]{1,0:T(8,128)S(1)}, f32[1024,1024]{1,0:T(8,128)}, u32[]{:S(2)}) copy-start(f32[1024,1024]{1,0:T(8,128)} %fusion.15) | copy-start | bytes 12582916

commit v2 on v1

--- a/solution.py
+++ b/solution.py
@@ -10,32 +10,47 @@
 HEAD_SIZE = 128
 BLOCK_TOKENS = 512
 ROW_TILE = 256
+MATES = 4
 EXPONENT_SCALE = HEAD_SIZE ** (-0.5) * 1.4426950408889634
 NT = (((1,), (1,)), ((), ()))
 
 
-def pack_kernel(block_ref, key_ref, value_ref, out_ref):
-    out_ref[0, :, :HEAD_SIZE] = key_ref[...]
-    out_ref[0, :, HEAD_SIZE:] = value_ref[...]
-
-
-def pack_head(local_block, keys, values, head):
-    count = local_block.shape[0]
-    spec = pl.BlockSpec((BLOCK_TOKENS, HEAD_SIZE), lambda i, block: (block[i], head))
+def pack_kernel(block_ref, *refs):
+    count = len(refs) // 2
+    for have, out in zip(refs[:count], refs[count:]):
+        out[...] = have[...]
+
+
+def pack_head(blocks, gathered):
+    mates, owners = blocks.shape
+
+    def pick(mate):
+        return pl.BlockSpec(
+            (1, BLOCK_TOKENS, 2 * HEAD_SIZE),
+            lambda i, block: (i, block[mate * owners + i], 0),
+        )
+
+    size = owners * BLOCK_TOKENS * 2 * HEAD_SIZE
     return pl.pallas_call(
         pack_kernel,
         grid_spec=pltpu.PrefetchScalarGridSpec(
             num_scalar_prefetch=1,
-            grid=(count,),
-            in_specs=[spec, spec],
-            out_specs=pl.BlockSpec((1, BLOCK_TOKENS, 2 * HEAD_SIZE), lambda i, block: (i, 0, 0)),
-        ),
-        out_shape=jax.ShapeDtypeStruct((count, BLOCK_TOKENS, 2 * HEAD_SIZE), jnp.bfloat16),
+            grid=(owners,),
+            in_specs=[pick(mate) for mate in range(mates)],
+            out_specs=[
+                pl.BlockSpec((1, BLOCK_TOKENS, 2 * HEAD_SIZE), lambda i, block: (i, 0, 0))
+            ]
+            * mates,
+        ),
+        out_shape=[
+            jax.ShapeDtypeStruct((owners, BLOCK_TOKENS, 2 * HEAD_SIZE), jnp.bfloat16)
+        ]
+        * mates,
         cost_estimate=pl.CostEstimate(
-            flops=0, bytes_accessed=count * BLOCK_TOKENS * 2 * HEAD_SIZE * 4, transcendentals=0
+            flops=0, bytes_accessed=size * mates * 4, transcendentals=0
         ),
         name="pack_head",
-    )(local_block, keys, values)
+    )(blocks.reshape(-1), *([gathered] * mates))
 
 
 def attention_kernel(
@@ -146,24 +161,37 @@
         share = lax.dynamic_slice_in_dim(out_weight, start, out_columns, axis=1)
         weights.append(share if s == 0 else lax.ppermute(share, "head", turns[s]))
 
+    owners = ctx_count // MATES
+    columns = [[z * MATES + q for z in range(owners)] for q in range(MATES)]
+    gathered = []
+    for head in range(kv_heads):
+        lanes = slice(head * HEAD_SIZE, (head + 1) * HEAD_SIZE)
+        pair = jnp.concatenate([keys[:, lanes], values[:, lanes]], axis=1)
+        gathered.append(lax.all_gather(pair, "ctx", axis_index_groups=columns, axis=0))
+
     wanted = selected.reshape(request_count)
     everyone = lax.all_gather(selected, "ctx", axis=0, tiled=True).reshape(ctx_count, request_count)
-    asked = jnp.max(jnp.where(everyone // blk_dev == ctx_index, everyone, -1), axis=1)
-    local_block = jnp.clip(asked - ctx_index * blk_dev, 0, blk_dev - 1).astype(jnp.int32)
-    source = jnp.clip(wanted // blk_dev, 0, ctx_count - 1).astype(jnp.int32)
+    mine = ctx_index % MATES
+    mates = jnp.bitwise_xor(ctx_index, jnp.arange(MATES))
+    asked = everyone[mates][:, None, :]
+    owner_ids = (jnp.arange(owners) * MATES + mine)[None, :, None]
+    asked = jnp.max(jnp.where(asked // blk_dev == owner_ids, asked, -1), axis=2)
+    blocks = jnp.where(asked >= 0, asked % blk_dev, 0).astype(jnp.int32)
+    source = jnp.clip(wanted // blk_dev, 0, ctx_count - 1)
+    source = (jnp.bitwise_xor(source % MATES, mine) * owners + source // MATES).astype(jnp.int32)
     live = (wanted >= 0).astype(jnp.int32)
-
-    arrived = []
-    for head in range(kv_heads):
-        outgoing = pack_head(local_block, keys, values, head)
-        arrived.append(
-            lax.all_to_all(outgoing, "ctx", split_axis=0, concat_axis=0, tiled=True)
-        )
-
-    def project(parts, head):
-        total = None
+    hops = [[(i, i ^ k) for i in range(ctx_count)] for k in range(MATES)]
+
+    def fetch(head, after):
+        have = gathered[head]
+        if after is not None:
+            have, _ = lax.optimization_barrier((have, after))
+        packed = pack_head(blocks, have)
+        return [packed[0]] + [lax.ppermute(packed[k], "ctx", hops[k]) for k in range(1, MATES)]
+
+    def project(total, parts, shares, head):
         rows = slice(head * width, (head + 1) * width)
-        for part, weight in zip(parts, weights):
+        for part, weight in zip(parts, shares):
             term = jnp.dot(part, weight[rows], preferred_element_type=jnp.float32)
             total = term if total is None else total + term
         return total
@@ -171,23 +199,40 @@
     def spread(attended):
         return [attended] + [lax.ppermute(attended, "head", turns[s]) for s in range(1, head_count)]
 
+    last = kv_heads - 1
+    fetched = [None] * kv_heads
+    fetched[0] = fetch(0, None)
+    if last > 0:
+        fetched[1] = fetch(1, None)
     total = None
-    for head in range(kv_heads - 1):
+    pending = None
+    for head in range(last):
+        arrived = jnp.concatenate(fetched[head], axis=0)
+        if head == 0:
+            arrived, *weights = lax.optimization_barrier((arrived, *weights))
+        attended = attend_head(source, live, queries, keys, values, arrived, head, group, 0, blk_dev)
+        if head + 2 <= last:
+            fetched[head + 2] = fetch(head + 2, attended)
+        if pending is not None:
+            total = lax.optimization_barrier(project(total, pending, weights, head - 1))
+        pending = spread(attended)
+    arrived = jnp.concatenate(fetched[last], axis=0)
+    if total is not None:
+        arrived, total = lax.optimization_barrier((arrived, total))
+    half = blk_dev // 2
+    parts = []
+    for first, count in ((0, half), (half, blk_dev - half)):
         attended = attend_head(
-            source, live, queries, keys, values, arrived[head], head, group, 0, blk_dev
+            source, live, queries, keys, values, arrived, last, group, first, count
         )
-        term = project(spread(attended), head)
-        total = term if total is None else total + term
-    head = kv_heads - 1
-    half = blk_dev // 2
+        parts.append((first, count, spread(attended)))
+    if pending is not None:
+        total = lax.optimization_barrier(project(total, pending, weights, last - 1))
     outputs = []
-    for first, blocks in ((0, half), (half, blk_dev - half)):
-        attended = attend_head(
-            source, live, queries, keys, values, arrived[head], head, group, first, blocks
-        )
-        term = project(spread(attended), head)
-        rows = slice(first * BLOCK_TOKENS, (first + blocks) * BLOCK_TOKENS)
-        outputs.append((term if total is None else total[rows] + term).astype(jnp.bfloat16))
+    for first, count, part in parts:
+        rows = slice(first * BLOCK_TOKENS, (first + count) * BLOCK_TOKENS)
+        before = None if total is None else total[rows]
+        outputs.append(project(before, part, weights, last).astype(jnp.bfloat16))
     return jnp.concatenate(outputs, axis=0)
 
 

time: 626 us -> 504 us (0.81)
  waiting for transfers between devices: 289 us -> 235 us
  starting transfers between devices: 69.7 us -> 18.2 us
  Pallas kernels: 147 us -> 122 us
  matrix products: 73.5 us -> 55.1 us
  between operations: 0.38 us -> 13.9 us
  other arithmetic: 3.3 us -> 14.9 us
    all_gather x0 -> x4, waiting for transfers between devices: none -> 206 us  [per_device(): lax.all_gather(pair, 'ctx', axis_index_groups=columns, axis=0)]
    all_to_all x4 -> x0, waiting for transfers between devices: 200 us -> none  [per_device(): lax.all_to_all(outgoing, 'ctx', split_axis=0, concat_axis=0, tiled=True)]
    ppermute x5, waiting for transfers between devices: 89.4 us -> 12.3 us  [spread(): lax.ppermute(attended, 'head', turns[s])]
    all_to_all x4 -> x0, starting transfers between devices: 63.6 us -> none  [per_device(): lax.all_to_all(outgoing, 'ctx', split_axis=0, concat_axis=0, tiled=True)]
    pallas_call x4, Pallas kernels: 44 us -> 23.1 us  [pack_head(): pl.pallas_call(pack_kernel, grid_spec=pltpu.PrefetchScalarGridSpec(num_sc...]
    dot_general x10, matrix products: 73.5 us -> 55.1 us  [project(): term = jnp.dot(part, weight[rows], preferred_element_type=jnp.float32)]
    ppermute x0 -> x12, waiting for transfers between devices: none -> 16.8 us  [fetch(): lax.ppermute(packed[k], 'ctx', hops[k])]
    concatenate x0 -> x8, other arithmetic: none -> 11.6 us  [the longest x3 6.53 us: per_device(): arrived = jnp.concatenate(fetched[head], axis=0)]
  transfers between devices with their start and end apart: 10 -> 22, of which waited for: 7 -> 6; matrix products, arithmetic and copies ran while one was open for 12% -> 15% of each run, Pallas kernels for 22% -> 25%
where the time goes in v2:
time: 504 us; the launch traced here: 496 us
  waiting for transfers between devices  235 us (47%)
  Pallas kernels  122 us (24%)
  matrix products  55.1 us (11%)
  blocking collectives  22.2 us (4%)
  starting transfers between devices  18.2 us (4%)
  other arithmetic  14.9 us (3%)
  local copies, waits for them, and re-layouts  14.4 us (3%)
  between operations  13.9 us (3%)
    all_gather x4, waiting for transfers between devices, per_device(): lax.all_gather(pair, 'ctx', axis_index_groups=columns, axis=0)  206 us
    pallas_call x5, Pallas kernels, attend_head(): pl.pallas_call(functools.partial(attention_kernel, first, group), grid_sp...  98.8 us
    dot_general x10, matrix products, project(): term = jnp.dot(part, weight[rows], preferred_element_type=jnp.float32)  55.1 us
    pallas_call x4, Pallas kernels, pack_head(): pl.pallas_call(pack_kernel, grid_spec=pltpu.PrefetchScalarGridSpec(num_sc...  23.1 us
    all_gather x1, blocking collectives, per_device(): lax.all_gather(selected, 'ctx', axis=0, tiled=True)  22.2 us
    ppermute x12, waiting for transfers between devices, fetch(): lax.ppermute(packed[k], 'ctx', hops[k])  16.8 us
    ppermute x5, waiting for transfers between devices, spread(): lax.ppermute(attended, 'head', turns[s])  12.3 us
  transfers between devices with their start and end apart: 22, of which 6 were waited for; matrix products, arithmetic and copies ran while one was open for 15% of the time, Pallas kernels for 25%

profile of v2, /device:TPU:0, one launch (start us, length us, event | category | flops | bytes accessed | tf_op | source)
XLA Modules:
  0.0 495.8 jit_solution(15695404824443144052)
XLA Ops:
  6.5 2.6 fusion.32
  9.1 1.1 pad_maximum_fusion.7
  10.3 1.1 pad_maximum_fusion.6
  11.5 1.1 pad_maximum_fusion.8
  12.7 7.9 %constant_dynamic-slice_fusion = (bf16[2048,1024]{1,0:T(8,128)(2,1)}, bf16[2048,1024]{1,0:T(8,128)(2,1)}) fusion(bf16[2048,2048]{1,0:T(8,128)(2,1)} %param.9, s32[]{:T(128)S(6)} %select_n.73, s32[]{:T(128)S(6)} %select_n.72), kind=kLoop, calls=%fused_computation.66 | loop fusion | bytes 16777224 | tf_op jit(solution)/shard_map/dynamic_slice | solution.py:161
  20.5 3.0 collective-permute-start.9
  23.5 1.1 pad_maximum_fusion.5
  24.6 22.2 %all-gather.4 = s32[16,4,3]{2,1,0:T(4,128)S(1)} all-gather(s32[1,4,3]{2,1,0:T(4,128)S(1)} %bitcast.35), channel_id=1, replica_groups=mesh['ctx'=16,'head'=2] {'ctx'}, dimensions={0}, use_global_device_ids=true | all-gather | bytes 816 | tf_op jit(solution)/shard_map/all_gather | solution.py:173
  46.9 0.6 gather_fusion
  47.5 0.2 select_reduce_fusion
  47.7 0.1 reduce_max.12
  47.8 0.6 compare_select_fusion.3.block_ref
  48.4 45.5 %all-gather.14.cloned.1.call-done = bf16[8192,256]{1,0:T(8,128)(2,1)} async-done(((bf16[2048,256]{1,0:T(8,128)(2,1)}), bf16[8192,256]{1,0:T(8,128)(2,1)}) %all-gather.14.cloned.1.call-update) | async-done | bytes 4194320 | tf_op jit(solution)/shard_map/all_gather | solution.py:170
  93.9 5.9 %pack_head.6 = (bf16[4,512,256]{2,1,0:T(8,128)(2,1)}, bf16[4,512,256]{2,1,0:T(8,128)(2,1)}, bf16[4,512,256]{2,1,0:T(8,128)(2,1)}, bf16[4,512,256]{2,1,0:T(8,128)(2,1)}) custom-call(s32[16]{0:T(128)} %compare_select_fusion.3.block_ref, bf16[4,2048,256]{2,1,0:T(8,128)(2,1)} %bitcast.29, bf16[4,2048,256]{2,1,0:T(8,128)(2,1)} %bitcast.30, ...), custom_call_target="tpu_custom_call" | custom-call | bytes 8388608 | tf_op jit(solution)/shard_map/pack_head/pallas_call | solution.py:34
  99.8 1.3 collective-permute-start.8
  101.1 0.5 collective-permute-start.7
  101.8 73.1 %all-gather.12.cloned.1.call-done = bf16[8192,256]{1,0:T(8,128)(2,1)} async-done(((bf16[2048,256]{1,0:T(8,128)(2,1)}), bf16[8192,256]{1,0:T(8,128)(2,1)}) %all-gather.12.cloned.1.call-update) | async-done | bytes 4194320 | tf_op jit(solution)/shard_map/all_gather | solution.py:170
  174.9 5.7 %pack_head.4 = (bf16[4,512,256]{2,1,0:T(8,128)(2,1)}, bf16[4,512,256]{2,1,0:T(8,128)(2,1)}, bf16[4,512,256]{2,1,0:T(8,128)(2,1)}, bf16[4,512,256]{2,1,0:T(8,128)(2,1)}) custom-call(s32[16]{0:T(128)} %compare_select_fusion.3.block_ref, bf16[4,2048,256]{2,1,0:T(8,128)(2,1)} %bitcast.25, bf16[4,2048,256]{2,1,0:T(8,128)(2,1)} %bitcast.26, ...), custom_call_target="tpu_custom_call" | custom-call | bytes 8388608 | tf_op jit(solution)/shard_map/pack_head/pallas_call | solution.py:34
  180.6 1.5 collective-permute-start.2
  182.1 0.5 collective-permute-start.1
  182.6 0.1 collective-permute-start
  182.8 1.8 pad_maximum_fusion.2.far0.far1.far2
  184.6 0.3 copy-done
  184.8 0.8 copy-done.3
  185.7 23.8 %attend_head.6 = bf16[2048,512]{1,0:T(8,128)(2,1)S(1)} custom-call(s32[12]{0:T(128)S(1)} %fusion.29.source_ref, s32[12]{0:T(128)S(1)} %compare_convert_fusion.live_ref, bf16[2048,2048]{1,0:T(8,128)(2,1)} %query_ref.9, bf16[2048,512]{1,0:T(8,128)(2,1)S(1)} %copy-done, bf16[2048,512]{1,0:T(8,128)(2,1)S(1)} %copy-done.3, ...), custom_call_target="tpu_custom_call" | custom-call | flops 17179869184 | bytes 8388608 | tf_op jit(solution)/shard_map/attend_head/pallas_call | solution.py:119
  209.5 1.6 collective-permute-start.10
  211.1 44.7 %all-gather.16.cloned.1.call-done = bf16[8192,256]{1,0:T(8,128)(2,1)} async-done(((bf16[2048,256]{1,0:T(8,128)(2,1)}), bf16[8192,256]{1,0:T(8,128)(2,1)}) %all-gather.16.cloned.1.call-update) | async-done | bytes 4194320 | tf_op jit(solution)/shard_map/all_gather | solution.py:170
  255.8 5.9 %pack_head.7 = (bf16[4,512,256]{2,1,0:T(8,128)(2,1)}, bf16[4,512,256]{2,1,0:T(8,128)(2,1)}, bf16[4,512,256]{2,1,0:T(8,128)(2,1)}, bf16[4,512,256]{2,1,0:T(8,128)(2,1)}) custom-call(s32[16]{0:T(128)} %compare_select_fusion.3.block_ref, bf16[4,2048,256]{2,1,0:T(8,128)(2,1)} %bitcast.17, bf16[4,2048,256]{2,1,0:T(8,128)(2,1)} %bitcast.18, ...), custom_call_target="tpu_custom_call" | custom-call | bytes 8388608 | tf_op jit(solution)/shard_map/pack_head/pallas_call | solution.py:34
  261.7 1.4 collective-permute-start.14
  263.1 0.5 collective-permute-start.13
  263.6 0.1 collective-permute-start.12
  263.8 2.5 pad_maximum_fusion.far0.far1.far2
  266.2 0.4 copy-done.1
  266.7 0.7 copy-done.4
  267.3 24.9 %attend_head.5 = bf16[2048,512]{1,0:T(8,128)(2,1)} custom-call(s32[12]{0:T(128)S(1)} %fusion.29.source_ref, s32[12]{0:T(128)S(1)} %compare_convert_fusion.live_ref, bf16[2048,2048]{1,0:T(8,128)(2,1)} %query_ref.9, bf16[2048,512]{1,0:T(8,128)(2,1)S(1)} %copy-done.1, bf16[2048,512]{1,0:T(8,128)(2,1)S(1)} %copy-done.4, ...), custom_call_target="tpu_custom_call" | custom-call | flops 17179869184 | bytes 8388608 | tf_op jit(solution)/shard_map/attend_head/pallas_call | solution.py:119
  292.2 1.6 collective-permute-start.11
  293.8 42.7 %all-gather.10.cloned.1.call-done = bf16[8192,256]{1,0:T(8,128)(2,1)} async-done(((bf16[2048,256]{1,0:T(8,128)(2,1)}), bf16[8192,256]{1,0:T(8,128)(2,1)}) %all-gather.10.cloned.1.call-update) | async-done | bytes 4194320 | tf_op jit(solution)/shard_map/all_gather | solution.py:170
  336.5 5.6 %pack_head.5 = (bf16[4,512,256]{2,1,0:T(8,128)(2,1)}, bf16[4,512,256]{2,1,0:T(8,128)(2,1)}, bf16[4,512,256]{2,1,0:T(8,128)(2,1)}, bf16[4,512,256]{2,1,0:T(8,128)(2,1)}) custom-call(s32[16]{0:T(128)} %compare_select_fusion.3.block_ref, bf16[4,2048,256]{2,1,0:T(8,128)(2,1)} %bitcast.21, bf16[4,2048,256]{2,1,0:T(8,128)(2,1)} %bitcast.22, ...), custom_call_target="tpu_custom_call" | custom-call | bytes 8388608 | tf_op jit(solution)/shard_map/pack_head/pallas_call | solution.py:34
  342.2 7.6 %fusion.14 = f32[2048,1024]{1,0:T(8,128)} fusion(bf16[2048,512]{1,0:T(8,128)(2,1)} %attend_head.5, bf16[2048,1024]{1,0:T(8,128)(2,1)} %get-tuple-element.42), kind=kOutput, calls=%fused_computation.25 | convolution fusion | flops 2147483648 | bytes 11534336 | tf_op jit(solution)/shard_map/dot_general | solution.py:195
  349.8 1.4 collective-permute-start.5
  351.2 0.6 collective-permute-start.4
  351.8 0.1 collective-permute-start.3
  351.9 2.3 pad_maximum_fusion.3.far0.far1.far2
  354.2 0.3 copy-done.2
  354.5 0.6 copy-done.5
  355.1 24.3 %attend_head.7 = bf16[2048,512]{1,0:T(8,128)(2,1)S(1)} custom-call(s32[12]{0:T(128)S(1)} %fusion.29.source_ref, s32[12]{0:T(128)S(1)} %compare_convert_fusion.live_ref, bf16[2048,2048]{1,0:T(8,128)(2,1)} %query_ref.9, bf16[2048,512]{1,0:T(8,128)(2,1)S(1)} %copy-done.2, bf16[2048,512]{1,0:T(8,128)(2,1)S(1)} %copy-done.5, ...), custom_call_target="tpu_custom_call" | custom-call | flops 17179869184 | bytes 8388608 | tf_op jit(solution)/shard_map/attend_head/pallas_call | solution.py:119
  379.4 1.6 collective-permute-start.15
  381.0 16.7 %collective-permute-done.4 = bf16[4,512,256]{2,1,0:T(8,128)(2,1)S(1)} collective-permute-done((bf16[4,512,256]{2,1,0:T(8,128)(2,1)S(1)}, bf16[4,512,256]{2,1,0:T(8,128)(2,1)S(1)}, u32[]{:S(2)}, u32[]{:S(2)}) %collective-permute-start.4) | collective-permute-done | bytes 1048608 | tf_op jit(solution)/shard_map/ppermute | solution.py:190
  397.7 0.7 pad_maximum_fusion.1.far0.far1.far2
  398.5 6.8 %fusion.8 = f32[2048,1024]{1,0:T(8,128)} fusion(bf16[2048,512]{1,0:T(8,128)(2,1)S(1)} %attend_head.7, bf16[2048,1024]{1,0:T(8,128)(2,1)} %get-tuple-element.42), kind=kOutput, calls=%fused_computation.21 | convolution fusion | flops 2147483648 | bytes 11534336 | tf_op jit(solution)/shard_map/dot_general | solution.py:195
  405.3 4.3 fusion.16
  409.6 3.8 convolution_add_fusion
  413.5 10.1 %add_add_fusion.1 = f32[2048,1024]{1,0:T(8,128)} fusion(f32[2048,1024]{1,0:T(8,128)S(1)} %convolution_add_fusion, f32[2048,1024]{1,0:T(8,128)} %fusion.14, bf16[2048,512]{1,0:T(8,128)(2,1)} %collective-permute-done.11, bf16[2048,1024]{1,0:T(8,128)(2,1)} %collective-permute-done.9), kind=kOutput, calls=%fused_computation.2 | convolution fusion | flops 2151677952 | bytes 28311552 | tf_op jit(solution)/shard_map/dot_general | solution.py:195
  423.5 12.9 %attend_head.9 = bf16[1024,512]{1,0:T(8,128)(2,1)S(1)} custom-call(s32[12]{0:T(128)S(1)} %fusion.29.source_ref, s32[12]{0:T(128)S(1)} %compare_convert_fusion.live_ref, bf16[2048,2048]{1,0:T(8,128)(2,1)} %query_ref.9, bf16[2048,512]{1,0:T(8,128)(2,1)S(1)} %copy-done.2, bf16[2048,512]{1,0:T(8,128)(2,1)S(1)} %copy-done.5, ...), custom_call_target="tpu_custom_call" | custom-call | flops 8589934592 | bytes 4194304 | tf_op jit(solution)/shard_map/attend_head/pallas_call | solution.py:119
  436.4 1.6 collective-permute-start.17
  438.0 12.9 %attend_head.8 = bf16[1024,512]{1,0:T(8,128)(2,1)S(1)} custom-call(s32[12]{0:T(128)S(1)} %fusion.29.source_ref, s32[12]{0:T(128)S(1)} %compare_convert_fusion.live_ref, bf16[2048,2048]{1,0:T(8,128)(2,1)} %query_ref.9, bf16[2048,512]{1,0:T(8,128)(2,1)S(1)} %copy-done.2, bf16[2048,512]{1,0:T(8,128)(2,1)S(1)} %copy-done.5, ...), custom_call_target="tpu_custom_call" | custom-call | flops 8589934592 | bytes 4194304 | tf_op jit(solution)/shard_map/attend_head/pallas_call | solution.py:119
  450.9 0.6 collective-permute-start.16
  451.5 4.6 fusion.21
  456.1 4.7 fusion.23
  460.8 6.8 %add_add_fusion = f32[2048,1024]{1,0:T(8,128)S(1)} fusion(f32[2048,1024]{1,0:T(8,128)S(1)} %bitcast.34, f32[2048,1024]{1,0:T(8,128)} %fusion.8, bf16[2048,512]{1,0:T(8,128)(2,1)} %collective-permute-done.15, bf16[2048,1024]{1,0:T(8,128)(2,1)} %collective-permute-done.9), kind=kOutput, calls=%fused_computation.1 | convolution fusion | flops 2151677952 | bytes 28311552 | tf_op jit(solution)/shard_map/dot_general | solution.py:195
  467.6 3.9 fusion.1
  471.5 12.3 %collective-permute-done.16 = bf16[1024,512]{1,0:T(8,128)(2,1)S(1)} collective-permute-done((bf16[1024,512]{1,0:T(8,128)(2,1)S(1)}, bf16[1024,512]{1,0:T(8,128)(2,1)S(1)}, u32[]{:S(2)}, u32[]{:S(2)}) %collective-permute-start.16) | collective-permute-done | bytes 1048608 | tf_op jit(solution)/shard_map/ppermute | solution.py:200
  483.8 2.5 fusion.3
  486.3 2.5 pad_maximum_fusion.4
  (62 shorter events, 0.6 us)
Async XLA Ops:
  6.5 87.3 %all-gather.14.cloned.1.call-start = ((), (), s32[]{:S(2)}) async-start(), calls=%async_computation.2 | async-start | bytes 5242880 | tf_op jit(solution)/shard_map/all_gather | solution.py:170
  10.2 164.7 %all-gather.12.cloned.1.call-start = ((), (), s32[]{:S(2)}) async-start(), calls=%async_computation.1 | async-start | bytes 5242880 | tf_op jit(solution)/shard_map/all_gather | solution.py:170
  11.4 244.4 %all-gather.16.cloned.1.call-start = ((), (), s32[]{:S(2)}) async-start(), calls=%async_computation.3 | async-start | bytes 5242880 | tf_op jit(solution)/shard_map/all_gather | solution.py:170
  12.6 324.0 %all-gather.10.cloned.1.call-start = ((), (), s32[]{:S(2)}) async-start(), calls=%async_computation | async-start | bytes 5242880 | tf_op jit(solution)/shard_map/all_gather | solution.py:170
  12.6 12.0 %copy-start.11 = (s32[4,3]{1,0:T(4,128)S(1)}, s32[4,3]{1,0:T(4,128)}, u32[]{:S(2)}) copy-start(s32[4,3]{1,0:T(4,128)} %param.8) | copy-start | bytes 148
  20.5 164.1 %collective-permute-start.9 = (bf16[2048,1024]{1,0:T(8,128)(2,1)}, bf16[2048,1024]{1,0:T(8,128)(2,1)}, u32[]{:S(2)}, u32[]{:S(2)}) collective-permute-start(bf16[2048,1024]{1,0:T(8,128)(2,1)} %get-tuple-element.51), channel_id=1, source_target_pairs={{0,1},{1,0},{2,3},{3,2},{4,5},{5,4},{6,7},{7,6},{8,9},{9,8},{10,11... | collective-permute-start | bytes 12582920 | tf_op jit(solution)/shard_map/ppermute | solution.py:162
  99.8 82.3 %collective-permute-start.8 = (bf16[4,512,256]{2,1,0:T(8,128)(2,1)}, bf16[4,512,256]{2,1,0:T(8,128)(2,1)S(1)}, u32[]{:S(2)}, u32[]{:S(2)}) collective-permute-start(bf16[4,512,256]{2,1,0:T(8,128)(2,1)} %get-tuple-element.40), channel_id=1, source_target_pairs={{0,6},{2,4},{4,2},{6,0},{8,14},{10,12},{12,10},{14,8},{16,22},{18,... | collective-permute-start | bytes 3145736 | tf_op jit(solution)/shard_map/ppermute | solution.py:190
  101.1 81.6 %collective-permute-start.7 = (bf16[4,512,256]{2,1,0:T(8,128)(2,1)}, bf16[4,512,256]{2,1,0:T(8,128)(2,1)S(1)}, u32[]{:S(2)}, u32[]{:S(2)}) collective-permute-start(bf16[4,512,256]{2,1,0:T(8,128)(2,1)} %get-tuple-element.39), channel_id=1, source_target_pairs={{0,4},{2,6},{4,0},{6,2},{8,12},{10,14},{12,8},{14,10},{16,20},{18,... | collective-permute-start | bytes 3145736 | tf_op jit(solution)/shard_map/ppermute | solution.py:190
  101.6 81.1 %collective-permute-start.6 = (bf16[4,512,256]{2,1,0:T(8,128)(2,1)}, bf16[4,512,256]{2,1,0:T(8,128)(2,1)}, u32[]{:S(2)}, u32[]{:S(2)}) collective-permute-start(bf16[4,512,256]{2,1,0:T(8,128)(2,1)} %get-tuple-element.38), channel_id=1, source_target_pairs={{0,2},{2,0},{4,6},{6,4},{8,10},{10,8},{12,14},{14,12},{16,18},{18,... | collective-permute-start | bytes 3145736 | tf_op jit(solution)/shard_map/ppermute | solution.py:190
  174.9 7.9 %copy-start.9 = (bf16[4,512,256]{2,1,0:T(8,128)(2,1)S(1)}, bf16[4,512,256]{2,1,0:T(8,128)(2,1)}, u32[]{:S(2)}) copy-start(bf16[4,512,256]{2,1,0:T(8,128)(2,1)} %get-tuple-element.37) | copy-start | bytes 3145732
  180.6 82.5 %collective-permute-start.2 = (bf16[4,512,256]{2,1,0:T(8,128)(2,1)}, bf16[4,512,256]{2,1,0:T(8,128)(2,1)}, u32[]{:S(2)}, u32[]{:S(2)}) collective-permute-start(bf16[4,512,256]{2,1,0:T(8,128)(2,1)} %get-tuple-element.31), channel_id=1, source_target_pairs={{0,6},{2,4},{4,2},{6,0},{8,14},{10,12},{12,10},{14,8},{16,22},{18,... | collective-permute-start | bytes 3145736 | tf_op jit(solution)/shard_map/ppermute | solution.py:190
  182.1 81.5 %collective-permute-start.1 = (bf16[4,512,256]{2,1,0:T(8,128)(2,1)}, bf16[4,512,256]{2,1,0:T(8,128)(2,1)}, u32[]{:S(2)}, u32[]{:S(2)}) collective-permute-start(bf16[4,512,256]{2,1,0:T(8,128)(2,1)} %get-tuple-element.30), channel_id=1, source_target_pairs={{0,4},{2,6},{4,0},{6,2},{8,12},{10,14},{12,8},{14,10},{16,20},{18,... | collective-permute-start | bytes 3145736 | tf_op jit(solution)/shard_map/ppermute | solution.py:190
  182.6 81.1 %collective-permute-start = (bf16[4,512,256]{2,1,0:T(8,128)(2,1)}, bf16[4,512,256]{2,1,0:T(8,128)(2,1)}, u32[]{:S(2)}, u32[]{:S(2)}) collective-permute-start(bf16[4,512,256]{2,1,0:T(8,128)(2,1)} %get-tuple-element.29), channel_id=1, source_target_pairs={{0,2},{2,0},{4,6},{6,4},{8,10},{10,8},{12,14},{14,12},{16,18},{18,... | collective-permute-start | bytes 3145736 | tf_op jit(solution)/shard_map/ppermute | solution.py:190
  182.8 2.1 copy-start
  182.8 2.9 copy-start.3
  209.5 195.9 %collective-permute-start.10 = (bf16[2048,512]{1,0:T(8,128)(2,1)S(1)}, bf16[2048,512]{1,0:T(8,128)(2,1)}, u32[]{:S(2)}, u32[]{:S(2)}) collective-permute-start(bf16[2048,512]{1,0:T(8,128)(2,1)S(1)} %attend_head.6), channel_id=1, source_target_pairs={{0,1},{1,0},{2,3},{3,2},{4,5},{5,4},{6,7},{7,6},{8,9},{9,8},{10,11... | collective-permute-start | bytes 6291464 | tf_op jit(solution)/shard_map/ppermute | solution.py:200
  255.8 8.0 %copy-start.7 = (bf16[4,512,256]{2,1,0:T(8,128)(2,1)S(1)}, bf16[4,512,256]{2,1,0:T(8,128)(2,1)}, u32[]{:S(2)}) copy-start(bf16[4,512,256]{2,1,0:T(8,128)(2,1)} %get-tuple-element.28) | copy-start | bytes 3145732
  261.7 88.1 %collective-permute-start.14 = (bf16[4,512,256]{2,1,0:T(8,128)(2,1)}, bf16[4,512,256]{2,1,0:T(8,128)(2,1)}, u32[]{:S(2)}, u32[]{:S(2)}) collective-permute-start(bf16[4,512,256]{2,1,0:T(8,128)(2,1)} %get-tuple-element.49), channel_id=1, source_target_pairs={{0,6},{2,4},{4,2},{6,0},{8,14},{10,12},{12,10},{14,8},{16,22},{18,... | collective-permute-start | bytes 3145736 | tf_op jit(solution)/shard_map/ppermute | solution.py:190
  263.1 88.1 %collective-permute-start.13 = (bf16[4,512,256]{2,1,0:T(8,128)(2,1)}, bf16[4,512,256]{2,1,0:T(8,128)(2,1)}, u32[]{:S(2)}, u32[]{:S(2)}) collective-permute-start(bf16[4,512,256]{2,1,0:T(8,128)(2,1)} %get-tuple-element.48), channel_id=1, source_target_pairs={{0,4},{2,6},{4,0},{6,2},{8,12},{10,14},{12,8},{14,10},{16,20},{18,... | collective-permute-start | bytes 3145736 | tf_op jit(solution)/shard_map/ppermute | solution.py:190
  263.6 88.2 %collective-permute-start.12 = (bf16[4,512,256]{2,1,0:T(8,128)(2,1)}, bf16[4,512,256]{2,1,0:T(8,128)(2,1)}, u32[]{:S(2)}, u32[]{:S(2)}) collective-permute-start(bf16[4,512,256]{2,1,0:T(8,128)(2,1)} %get-tuple-element.47), channel_id=1, source_target_pairs={{0,2},{2,0},{4,6},{6,4},{8,10},{10,8},{12,14},{14,12},{16,18},{18,... | collective-permute-start | bytes 3145736 | tf_op jit(solution)/shard_map/ppermute | solution.py:190
  263.7 2.9 copy-start.1
  263.7 3.6 copy-start.4
  292.2 121.2 %collective-permute-start.11 = (bf16[2048,512]{1,0:T(8,128)(2,1)}, bf16[2048,512]{1,0:T(8,128)(2,1)}, u32[]{:S(2)}, u32[]{:S(2)}) collective-permute-start(bf16[2048,512]{1,0:T(8,128)(2,1)} %attend_head.5), channel_id=1, source_target_pairs={{0,1},{1,0},{2,3},{3,2},{4,5},{5,4},{6,7},{7,6},{8,9},{9,8},{10,11... | collective-permute-start | bytes 6291464 | tf_op jit(solution)/shard_map/ppermute | solution.py:200
  342.1 7.7 %copy-start.14 = (bf16[4,512,256]{2,1,0:T(8,128)(2,1)S(1)}, bf16[4,512,256]{2,1,0:T(8,128)(2,1)}, u32[]{:S(2)}) copy-start(bf16[4,512,256]{2,1,0:T(8,128)(2,1)} %get-tuple-element.36) | copy-start | bytes 3145732
  342.1 9.1 %copy-start.13 = (bf16[4,512,256]{2,1,0:T(8,128)(2,1)S(1)}, bf16[4,512,256]{2,1,0:T(8,128)(2,1)}, u32[]{:S(2)}) copy-start(bf16[4,512,256]{2,1,0:T(8,128)(2,1)} %get-tuple-element.35) | copy-start | bytes 3145732
  342.1 9.7 %copy-start.12 = (bf16[4,512,256]{2,1,0:T(8,128)(2,1)S(1)}, bf16[4,512,256]{2,1,0:T(8,128)(2,1)}, u32[]{:S(2)}) copy-start(bf16[4,512,256]{2,1,0:T(8,128)(2,1)} %get-tuple-element.34) | copy-start | bytes 3145732
  342.1 9.8 %copy-start.8 = (bf16[4,512,256]{2,1,0:T(8,128)(2,1)S(1)}, bf16[4,512,256]{2,1,0:T(8,128)(2,1)}, u32[]{:S(2)}) copy-start(bf16[4,512,256]{2,1,0:T(8,128)(2,1)} %get-tuple-element.46) | copy-start | bytes 3145732
  349.8 29.6 %collective-permute-start.5 = (bf16[4,512,256]{2,1,0:T(8,128)(2,1)S(1)}, bf16[4,512,256]{2,1,0:T(8,128)(2,1)S(1)}, u32[]{:S(2)}, u32[]{:S(2)}) collective-permute-start(bf16[4,512,256]{2,1,0:T(8,128)(2,1)S(1)} %copy-done.14), channel_id=1, source_target_pairs={{0,6},{2,4},{4,2},{6,0},{8,14},{10,12},{12,10},{14,8},{16,22},{18,... | collective-permute-start | bytes 3145736 | tf_op jit(solution)/shard_map/ppermute | solution.py:190
  351.2 46.5 %collective-permute-start.4 = (bf16[4,512,256]{2,1,0:T(8,128)(2,1)S(1)}, bf16[4,512,256]{2,1,0:T(8,128)(2,1)S(1)}, u32[]{:S(2)}, u32[]{:S(2)}) collective-permute-start(bf16[4,512,256]{2,1,0:T(8,128)(2,1)S(1)} %copy-done.13), channel_id=1, source_target_pairs={{0,4},{2,6},{4,0},{6,2},{8,12},{10,14},{12,8},{14,10},{16,20},{18,... | collective-permute-start | bytes 3145736 | tf_op jit(solution)/shard_map/ppermute | solution.py:190
  351.8 45.9 %collective-permute-start.3 = (bf16[4,512,256]{2,1,0:T(8,128)(2,1)S(1)}, bf16[4,512,256]{2,1,0:T(8,128)(2,1)S(1)}, u32[]{:S(2)}, u32[]{:S(2)}) collective-permute-start(bf16[4,512,256]{2,1,0:T(8,128)(2,1)S(1)} %copy-done.12), channel_id=1, source_target_pairs={{0,2},{2,0},{4,6},{6,4},{8,10},{10,8},{12,14},{14,12},{16,18},{18,... | collective-permute-start | bytes 3145736 | tf_op jit(solution)/shard_map/ppermute | solution.py:190
  351.9 2.5 copy-start.2
  351.9 3.2 copy-start.5
  355.1 42.6 %copy-start.10 = (bf16[4,512,256]{2,1,0:T(8,128)(2,1)S(1)}, bf16[4,512,256]{2,1,0:T(8,128)(2,1)}, u32[]{:S(2)}) copy-start(bf16[4,512,256]{2,1,0:T(8,128)(2,1)} %get-tuple-element.33) | copy-start | bytes 3145732
  379.4 81.4 %collective-permute-start.15 = (bf16[2048,512]{1,0:T(8,128)(2,1)S(1)}, bf16[2048,512]{1,0:T(8,128)(2,1)}, u32[]{:S(2)}, u32[]{:S(2)}) collective-permute-start(bf16[2048,512]{1,0:T(8,128)(2,1)S(1)} %attend_head.7), channel_id=1, source_target_pairs={{0,1},{1,0},{2,3},{3,2},{4,5},{5,4},{6,7},{7,6},{8,9},{9,8},{10,11... | collective-permute-start | bytes 6291464 | tf_op jit(solution)/shard_map/ppermute | solution.py:200
  436.4 31.2 %collective-permute-start.17 = (bf16[1024,512]{1,0:T(8,128)(2,1)S(1)}, bf16[1024,512]{1,0:T(8,128)(2,1)S(1)}, u32[]{:S(2)}, u32[]{:S(2)}) collective-permute-start(bf16[1024,512]{1,0:T(8,128)(2,1)S(1)} %attend_head.9), channel_id=1, source_target_pairs={{0,1},{1,0},{2,3},{3,2},{4,5},{5,4},{6,7},{7,6},{8,9},{9,8},{10,11... | collective-permute-start | bytes 3145736 | tf_op jit(solution)/shard_map/ppermute | solution.py:200
  450.9 33.0 %collective-permute-start.16 = (bf16[1024,512]{1,0:T(8,128)(2,1)S(1)}, bf16[1024,512]{1,0:T(8,128)(2,1)S(1)}, u32[]{:S(2)}, u32[]{:S(2)}) collective-permute-start(bf16[1024,512]{1,0:T(8,128)(2,1)S(1)} %attend_head.8), channel_id=1, source_target_pairs={{0,1},{1,0},{2,3},{3,2},{4,5},{5,4},{6,7},{7,6},{8,9},{9,8},{10,11... | collective-permute-start | bytes 3145736 | tf_op jit(solution)/shard_map/ppermute | solution.py:200
  451.5 9.3 %slice-start = ((s8[8388608]{0:T(1024)(128)(4,1)}), s8[4194304]{0:T(1024)(128)(4,1)S(1)}, s32[]{:S(2)}) async-start(s8[8388608]{0:T(1024)(128)(4,1)} %bitcast.33), calls=%async_computation.4 | async-start | bytes 8388608
  456.1 4.7 slice-start.1
  467.6 16.3 %copy-start.6 = (f32[1024,1024]{1,0:T(8,128)S(1)}, f32[1024,1024]{1,0:T(8,128)}, u32[]{:S(2)}) copy-start(f32[1024,1024]{1,0:T(8,128)} %fusion.23) | copy-start | bytes 12582916
Sparse Core Ops, SparseCore 0:
  10.3 83.4 all-gather.13
  95.4 79.4 all-gather.11
  176.5 79.2 all-gather.15
  257.2 79.2 all-gather.9

commit v3 on v2

--- a/solution.py
+++ b/solution.py
@@ -163,11 +163,21 @@
 
     owners = ctx_count // MATES
     columns = [[z * MATES + q for z in range(owners)] for q in range(MATES)]
-    gathered = []
+    chained = kv_heads - 1 if kv_heads > 2 else None
+    gathered = [None] * kv_heads
     for head in range(kv_heads):
         lanes = slice(head * HEAD_SIZE, (head + 1) * HEAD_SIZE)
         pair = jnp.concatenate([keys[:, lanes], values[:, lanes]], axis=1)
-        gathered.append(lax.all_gather(pair, "ctx", axis_index_groups=columns, axis=0))
+        if head == chained:
+            chain = [pair]
+            for s in range(1, owners):
+                up = [(i, i + MATES) for i in range((s - 1) * MATES, ctx_count - MATES)]
+                chain.append(lax.ppermute(chain[-1], "ctx", up))
+        else:
+            gathered[head] = lax.all_gather(pair, "ctx", axis_index_groups=columns, axis=0)
+    if chained is not None:
+        gathered[0], *chain = lax.optimization_barrier((gathered[0], *chain))
+        gathered[chained] = jnp.stack(chain, axis=0)
 
     wanted = selected.reshape(request_count)
     everyone = lax.all_gather(selected, "ctx", axis=0, tiled=True).reshape(ctx_count, request_count)
@@ -177,8 +187,14 @@
     owner_ids = (jnp.arange(owners) * MATES + mine)[None, :, None]
     asked = jnp.max(jnp.where(asked // blk_dev == owner_ids, asked, -1), axis=2)
     blocks = jnp.where(asked >= 0, asked % blk_dev, 0).astype(jnp.int32)
-    source = jnp.clip(wanted // blk_dev, 0, ctx_count - 1)
-    source = (jnp.bitwise_xor(source % MATES, mine) * owners + source // MATES).astype(jnp.int32)
+    place = ctx_index // MATES
+    upward = lax.rem(place - jnp.arange(owners) + owners, owners)
+    chain_blocks = blocks[:, upward]
+    wanted_owner = jnp.clip(wanted // blk_dev, 0, ctx_count - 1)
+    sender = jnp.bitwise_xor(wanted_owner % MATES, mine) * owners
+    source = (sender + wanted_owner // MATES).astype(jnp.int32)
+    distance = lax.rem(place - wanted_owner // MATES + owners, owners)
+    chain_source = (sender + distance).astype(jnp.int32)
     live = (wanted >= 0).astype(jnp.int32)
     hops = [[(i, i ^ k) for i in range(ctx_count)] for k in range(MATES)]
 
@@ -186,7 +202,7 @@
         have = gathered[head]
         if after is not None:
             have, _ = lax.optimization_barrier((have, after))
-        packed = pack_head(blocks, have)
+        packed = pack_head(chain_blocks if head == chained else blocks, have)
         return [packed[0]] + [lax.ppermute(packed[k], "ctx", hops[k]) for k in range(1, MATES)]
 
     def project(total, parts, shares, head):
@@ -199,35 +215,42 @@
     def spread(attended):
         return [attended] + [lax.ppermute(attended, "head", turns[s]) for s in range(1, head_count)]
 
-    last = kv_heads - 1
-    fetched = [None] * kv_heads
-    fetched[0] = fetch(0, None)
-    if last > 0:
-        fetched[1] = fetch(1, None)
+    def attend(head, arrived, first, count):
+        places = chain_source if head == chained else source
+        return attend_head(places, live, queries, keys, values, arrived, head, group, first, count)
+
+    order = list(range(kv_heads))
+    if chained is not None:
+        order = [0, chained] + list(range(1, chained))
+    last = order[-1]
+    fetched = {order[0]: fetch(order[0], None)}
+    if chained is not None:
+        fetched[chained] = fetch(chained, None)
     total = None
-    pending = None
-    for head in range(last):
+    pending = []
+    previous = None
+    for head in order[:-1]:
+        if head not in fetched:
+            fetched[head] = fetch(head, previous)
         arrived = jnp.concatenate(fetched[head], axis=0)
-        if head == 0:
+        if previous is None:
             arrived, *weights = lax.optimization_barrier((arrived, *weights))
-        attended = attend_head(source, live, queries, keys, values, arrived, head, group, 0, blk_dev)
-        if head + 2 <= last:
-            fetched[head + 2] = fetch(head + 2, attended)
-        if pending is not None:
-            total = lax.optimization_barrier(project(total, pending, weights, head - 1))
-        pending = spread(attended)
+        elif len(pending) > 1:
+            total = project(total, pending[0][1], weights, pending[0][0])
+            pending = pending[1:]
+            arrived, total = lax.optimization_barrier((arrived, total))
+        previous = attend(head, arrived, 0, blk_dev)
+        pending.append((head, spread(previous)))
+    if last not in fetched:
+        fetched[last] = fetch(last, previous)
     arrived = jnp.concatenate(fetched[last], axis=0)
-    if total is not None:
+    for head, part in pending:
+        total = project(total, part, weights, head)
         arrived, total = lax.optimization_barrier((arrived, total))
     half = blk_dev // 2
     parts = []
     for first, count in ((0, half), (half, blk_dev - half)):
-        attended = attend_head(
-            source, live, queries, keys, values, arrived, last, group, first, count
-        )
-        parts.append((first, count, spread(attended)))
-    if pending is not None:
-        total = lax.optimization_barrier(project(total, pending, weights, last - 1))
+        parts.append((first, count, spread(attend(last, arrived, first, count))))
     outputs = []
     for first, count, part in parts:
         rows = slice(first * BLOCK_TOKENS, (first + count) * BLOCK_TOKENS)

time: 504 us -> 592 us (1.17)
  blocking collectives: 22.2 us -> 162 us
  waiting for transfers between devices: 235 us -> 177 us
  starting transfers between devices: 18.2 us -> 27.1 us
    all_gather x4 -> x3, waiting for transfers between devices: 206 us -> 0.01 us  [per_device(): lax.all_gather(pair, 'ctx', axis_index_groups=columns, axis=0)]
    all_gather x1, blocking collectives: 22.2 us -> 162 us  [per_device(): lax.all_gather(selected, 'ctx', axis=0, tiled=True)]
    ppermute x12, waiting for transfers between devices: 16.8 us -> 121 us  [fetch(): lax.ppermute(packed[k], 'ctx', hops[k])]
    ppermute x0 -> x3, waiting for transfers between devices: none -> 30.8 us  [per_device(): chain.append(lax.ppermute(chain[-1], 'ctx', up))]
    ppermute x5, waiting for transfers between devices: 12.3 us -> 24.8 us  [spread(): lax.ppermute(attended, 'head', turns[s])]
    ppermute x0 -> x3, starting transfers between devices: none -> 7.35 us  [per_device(): chain.append(lax.ppermute(chain[-1], 'ctx', up))]
  transfers between devices with their start and end apart: 22 -> 24, of which waited for: 6 -> 10; matrix products, arithmetic and copies ran while one was open for 15% -> 11% of each run, Pallas kernels for 25% -> 19%
where the time goes in v3:
time: 592 us; the launch traced here: 584 us
  waiting for transfers between devices  177 us (30%)
  blocking collectives  162 us (27%)
  Pallas kernels  122 us (21%)
  matrix products  52.2 us (9%)
  starting transfers between devices  27.1 us (5%)
  local copies, waits for them, and re-layouts  15.1 us (3%)
  other arithmetic  15 us (3%)
  between operations  13.9 us (2%)
    all_gather x1, blocking collectives, per_device(): lax.all_gather(selected, 'ctx', axis=0, tiled=True)  162 us
    ppermute x12, waiting for transfers between devices, fetch(): lax.ppermute(packed[k], 'ctx', hops[k])  121 us
    pallas_call x5, Pallas kernels, attend_head(): pl.pallas_call(functools.partial(attention_kernel, first, group), grid_sp...  98.6 us
    dot_general x10, matrix products, project(): term = jnp.dot(part, weight[rows], preferred_element_type=jnp.float32)  52.2 us
    ppermute x3, waiting for transfers between devices, per_device(): chain.append(lax.ppermute(chain[-1], 'ctx', up))  30.8 us
    ppermute x5, waiting for transfers between devices, spread(): lax.ppermute(attended, 'head', turns[s])  24.8 us
    pallas_call x4, Pallas kernels, pack_head(): pl.pallas_call(pack_kernel, grid_spec=pltpu.PrefetchScalarGridSpec(num_sc...  23 us
  transfers between devices with their start and end apart: 24, of which 10 were waited for; matrix products, arithmetic and copies ran while one was open for 11% of the time, Pallas kernels for 19%

profile of v3, /device:TPU:0, one launch (start us, length us, event | category | flops | bytes accessed | tf_op | source)
XLA Modules:
  0.0 583.7 jit_solution(1269495444231199491)
XLA Ops:
  6.5 2.5 fusion.32
  9.1 1.1 pad_maximum_fusion.8
  10.2 1.1 pad_maximum_fusion.7
  11.5 5.0 collective-permute-start
  16.6 8.1 %constant_dynamic-slice_fusion = (bf16[2048,1024]{1,0:T(8,128)(2,1)}, bf16[2048,1024]{1,0:T(8,128)(2,1)}) fusion(bf16[2048,2048]{1,0:T(8,128)(2,1)} %param.9, s32[]{:T(128)S(6)} %select_n.96, s32[]{:T(128)S(6)} %select_n.95), kind=kLoop, calls=%fused_computation.78 | loop fusion | bytes 16777224 | tf_op jit(solution)/shard_map/dynamic_slice | solution.py:161
  24.7 1.4 collective-permute-start.12
  26.1 30.8 %collective-permute-done = bf16[2048,256]{1,0:T(8,128)(2,1)S(1)} collective-permute-done((bf16[2048,256]{1,0:T(8,128)(2,1)S(1)}, bf16[2048,256]{1,0:T(8,128)(2,1)S(1)}, u32[]{:S(2)}, u32[]{:S(2)}) %collective-permute-start) | collective-permute-done | bytes 1048608 | tf_op jit(solution)/shard_map/ppermute | solution.py:175
  56.9 1.6 collective-permute-start.1
  58.5 1.1 pad_maximum_fusion.6
  59.6 0.7 collective-permute-start.2
  60.5 162.1 %all-gather.3 = s32[16,4,3]{2,1,0:T(4,128)S(1)} all-gather(s32[1,4,3]{2,1,0:T(4,128)S(1)} %bitcast.38), channel_id=1, replica_groups=mesh['ctx'=16,'head'=2] {'ctx'}, dimensions={0}, use_global_device_ids=true | all-gather | bytes 816 | tf_op jit(solution)/shard_map/all_gather | solution.py:183
  222.7 0.6 gather_fusion
  223.7 0.5 compare_select_fusion.8.block_ref
  224.2 5.7 pack_head.6
  229.9 3.1 collective-permute-start.11
  233.2 0.6 gather_fusion.1
  233.8 0.6 reshape.109.block_ref
  234.5 3.4 pad_maximum_fusion.refs_0_.refs_1_.refs_2_.refs_3_
  237.9 6.0 %pack_head.4 = (bf16[4,512,256]{2,1,0:T(8,128)(2,1)}, bf16[4,512,256]{2,1,0:T(8,128)(2,1)}, bf16[4,512,256]{2,1,0:T(8,128)(2,1)}, bf16[4,512,256]{2,1,0:T(8,128)(2,1)}) custom-call(s32[16]{0:T(128)} %reshape.109.block_ref, bf16[4,2048,256]{2,1,0:T(8,128)(2,1)} %pad_maximum_fusion.refs_0_.refs_1_.refs_2_.refs_3_, ...), custom_call_target="tpu_custom_call" | custom-call | bytes 8388608 | tf_op jit(solution)/shard_map/pack_head/pallas_call | solution.py:34
  243.9 2.5 collective-permute-start.5
  246.3 10.5 %collective-permute-done.11 = bf16[4,512,256]{2,1,0:T(8,128)(2,1)} collective-permute-done((bf16[4,512,256]{2,1,0:T(8,128)(2,1)}, bf16[4,512,256]{2,1,0:T(8,128)(2,1)}, u32[]{:S(2)}, u32[]{:S(2)}) %collective-permute-start.11) | collective-permute-done | bytes 1048608 | tf_op jit(solution)/shard_map/ppermute | solution.py:206
  256.8 1.4 collective-permute-start.4
  258.2 21.6 %collective-permute-done.10 = bf16[4,512,256]{2,1,0:T(8,128)(2,1)} collective-permute-done((bf16[4,512,256]{2,1,0:T(8,128)(2,1)}, bf16[4,512,256]{2,1,0:T(8,128)(2,1)}, u32[]{:S(2)}, u32[]{:S(2)}) %collective-permute-start.10) | collective-permute-done | bytes 1048608 | tf_op jit(solution)/shard_map/ppermute | solution.py:206
  279.8 2.3 pad_maximum_fusion.3.far0.far1.far2
  282.1 0.2 copy-done
  282.4 0.6 copy-done.3
  283.0 23.8 %attend_head.6 = bf16[2048,512]{1,0:T(8,128)(2,1)S(1)} custom-call(s32[12]{0:T(128)S(1)} %add.119.source_ref, s32[12]{0:T(128)S(1)} %compare_convert_fusion.live_ref, bf16[2048,2048]{1,0:T(8,128)(2,1)} %query_ref.9, bf16[2048,512]{1,0:T(8,128)(2,1)S(1)} %copy-done, bf16[2048,512]{1,0:T(8,128)(2,1)S(1)} %copy-done.3, ...), custom_call_target="tpu_custom_call" | custom-call | flops 17179869184 | bytes 8388608 | tf_op jit(solution)/shard_map/attend_head/pallas_call | solution.py:119
  306.8 1.7 collective-permute-start.13
  308.5 15.9 %collective-permute-done.4 = bf16[4,512,256]{2,1,0:T(8,128)(2,1)S(1)} collective-permute-done((bf16[4,512,256]{2,1,0:T(8,128)(2,1)}, bf16[4,512,256]{2,1,0:T(8,128)(2,1)S(1)}, u32[]{:S(2)}, u32[]{:S(2)}) %collective-permute-start.4) | collective-permute-done | bytes 1048608 | tf_op jit(solution)/shard_map/ppermute | solution.py:206
  324.3 0.5 pad_maximum_fusion.1.far0.far1.far2
  324.9 24.3 %attend_head.5 = bf16[2048,512]{1,0:T(8,128)(2,1)S(1)} custom-call(s32[12]{0:T(128)S(1)} %get-tuple-element.69.source_ref, s32[12]{0:T(128)S(1)} %compare_convert_fusion.live_ref, bf16[2048,2048]{1,0:T(8,128)(2,1)} %query_ref.9, bf16[2048,512]{1,0:T(8,128)(2,1)S(1)} %copy-done, bf16[2048,512]{1,0:T(8,128)(2,1)S(1)} %copy-done.3, ...), custom_call_target="tpu_custom_call" | custom-call | flops 17179869184 | bytes 8388608 | tf_op jit(solution)/shard_map/attend_head/pallas_call | solution.py:119
  349.2 1.3 copy-done.6
  350.5 5.7 pack_head.5
  356.2 1.1 collective-permute-start.8
  357.3 0.7 collective-permute-start.7
  358.1 1.6 collective-permute-start.17
  359.7 21.9 %collective-permute-done.8 = bf16[4,512,256]{2,1,0:T(8,128)(2,1)S(1)} collective-permute-done((bf16[4,512,256]{2,1,0:T(8,128)(2,1)}, bf16[4,512,256]{2,1,0:T(8,128)(2,1)S(1)}, u32[]{:S(2)}, u32[]{:S(2)}) %collective-permute-start.8) | collective-permute-done | bytes 1048608 | tf_op jit(solution)/shard_map/ppermute | solution.py:206
  381.6 22.7 %collective-permute-done.7 = bf16[4,512,256]{2,1,0:T(8,128)(2,1)S(1)} collective-permute-done((bf16[4,512,256]{2,1,0:T(8,128)(2,1)}, bf16[4,512,256]{2,1,0:T(8,128)(2,1)S(1)}, u32[]{:S(2)}, u32[]{:S(2)}) %collective-permute-start.7) | collective-permute-done | bytes 1048608 | tf_op jit(solution)/shard_map/ppermute | solution.py:206
  404.3 1.6 pad_maximum_fusion.2.far0.far1.far2
  406.0 4.5 fusion.9
  410.5 5.8 convolution_add_fusion
  416.3 24.8 %attend_head.7 = bf16[2048,512]{1,0:T(8,128)(2,1)} custom-call(s32[12]{0:T(128)S(1)} %add.119.source_ref, s32[12]{0:T(128)S(1)} %compare_convert_fusion.live_ref, bf16[2048,2048]{1,0:T(8,128)(2,1)} %query_ref.9, bf16[2048,512]{1,0:T(8,128)(2,1)S(1)} %copy-done.1, bf16[2048,512]{1,0:T(8,128)(2,1)S(1)} %copy-done.4, ...), custom_call_target="tpu_custom_call" | custom-call | flops 17179869184 | bytes 8388608 | tf_op jit(solution)/shard_map/attend_head/pallas_call | solution.py:119
  441.1 1.6 collective-permute-start.18
  442.7 5.6 fusion.7
  448.3 5.6 pack_head.7
  453.9 2.0 collective-permute-start.16
  455.9 0.2 collective-permute-start.15
  456.2 7.6 %fusion.1 = f32[2048,1024]{1,0:T(8,128)} fusion(bf16[2048,512]{1,0:T(8,128)(2,1)} %attend_head.7, bf16[2048,1024]{1,0:T(8,128)(2,1)} %get-tuple-element.56), kind=kOutput, calls=%fused_computation.18 | convolution fusion | flops 2147483648 | bytes 11534336 | tf_op jit(solution)/shard_map/dot_general | solution.py:211
  463.8 10.1 %add_add_fusion.1 = f32[2048,1024]{1,0:T(8,128)} fusion(f32[2048,1024]{1,0:T(8,128)} %convolution_add_fusion, f32[2048,1024]{1,0:T(8,128)S(1)} %copy-done.8, bf16[2048,512]{1,0:T(8,128)(2,1)} %collective-permute-done.17, bf16[2048,1024]{1,0:T(8,128)(2,1)} %collective-permute-done.12), kind=kOutput, calls=%fused_computation.3 | convolution fusion | flops 2151677952 | bytes 28311552 | tf_op jit(solution)/shard_map/dot_general | solution.py:211
  473.9 5.7 collective-permute-done.16
  479.7 22.6 %collective-permute-done.15 = bf16[4,512,256]{2,1,0:T(8,128)(2,1)S(1)} collective-permute-done((bf16[4,512,256]{2,1,0:T(8,128)(2,1)}, bf16[4,512,256]{2,1,0:T(8,128)(2,1)S(1)}, u32[]{:S(2)}, u32[]{:S(2)}) %collective-permute-start.15) | collective-permute-done | bytes 1048608 | tf_op jit(solution)/shard_map/ppermute | solution.py:206
  502.3 0.5 pad_maximum_fusion.4.far0.far1.far2
  502.9 8.6 %add_add_fusion = f32[2048,1024]{1,0:T(8,128)S(1)} fusion(f32[2048,1024]{1,0:T(8,128)} %add_add_fusion.1, f32[2048,1024]{1,0:T(8,128)} %fusion.1, bf16[2048,512]{1,0:T(8,128)(2,1)S(1)} %collective-permute-done.18, bf16[2048,1024]{1,0:T(8,128)(2,1)} %collective-permute-done.12), kind=kOutput, calls=%fused_computation.2 | convolution fusion | flops 2151677952 | bytes 28311552 | tf_op jit(solution)/shard_map/dot_general | solution.py:211
  511.6 12.9 %attend_head.9 = bf16[1024,512]{1,0:T(8,128)(2,1)S(1)} custom-call(s32[12]{0:T(128)S(1)} %add.119.source_ref, s32[12]{0:T(128)S(1)} %compare_convert_fusion.live_ref, bf16[2048,2048]{1,0:T(8,128)(2,1)} %query_ref.9, bf16[2048,512]{1,0:T(8,128)(2,1)S(1)} %copy-done.2, bf16[2048,512]{1,0:T(8,128)(2,1)S(1)} %copy-done.5, ...), custom_call_target="tpu_custom_call" | custom-call | flops 8589934592 | bytes 4194304 | tf_op jit(solution)/shard_map/attend_head/pallas_call | solution.py:119
  524.4 0.5 collective-permute-start.20
  524.9 12.9 %attend_head.8 = bf16[1024,512]{1,0:T(8,128)(2,1)S(1)} custom-call(s32[12]{0:T(128)S(1)} %add.119.source_ref, s32[12]{0:T(128)S(1)} %compare_convert_fusion.live_ref, bf16[2048,2048]{1,0:T(8,128)(2,1)} %query_ref.9, bf16[2048,512]{1,0:T(8,128)(2,1)S(1)} %copy-done.2, bf16[2048,512]{1,0:T(8,128)(2,1)S(1)} %copy-done.5, ...), custom_call_target="tpu_custom_call" | custom-call | flops 8589934592 | bytes 4194304 | tf_op jit(solution)/shard_map/attend_head/pallas_call | solution.py:119
  537.8 1.7 collective-permute-start.19
  539.5 2.5 fusion.14
  542.0 2.5 fusion.16
  544.5 6.1 %collective-permute-done.20 = bf16[1024,512]{1,0:T(8,128)(2,1)S(1)} collective-permute-done((bf16[1024,512]{1,0:T(8,128)(2,1)S(1)}, bf16[1024,512]{1,0:T(8,128)(2,1)S(1)}, u32[]{:S(2)}, u32[]{:S(2)}) %collective-permute-start.20) | collective-permute-done | bytes 1048608 | tf_op jit(solution)/shard_map/ppermute | solution.py:216
  550.6 2.5 add_convert_fusion
  553.0 18.7 %collective-permute-done.19 = bf16[1024,512]{1,0:T(8,128)(2,1)S(1)} collective-permute-done((bf16[1024,512]{1,0:T(8,128)(2,1)S(1)}, bf16[1024,512]{1,0:T(8,128)(2,1)S(1)}, u32[]{:S(2)}, u32[]{:S(2)}) %collective-permute-start.19) | collective-permute-done | bytes 1048608 | tf_op jit(solution)/shard_map/ppermute | solution.py:216
  571.8 2.5 add_convert_fusion.1
  574.2 2.5 pad_maximum_fusion.5
  (67 shorter events, 1.4 us)
Async XLA Ops:
  6.5 217.7 %all-gather.12.cloned.1.call-start = ((), (), s32[]{:S(2)}) async-start(), calls=%async_computation.2 | async-start | bytes 5242880 | tf_op jit(solution)/shard_map/all_gather | solution.py:177
  10.2 340.3 %all-gather.10.cloned.1.call-start = ((), (), s32[]{:S(2)}) async-start(), calls=%async_computation.1 | async-start | bytes 5242880 | tf_op jit(solution)/shard_map/all_gather | solution.py:177
  11.4 436.9 %all-gather.8.cloned.1.call-start = ((), (), s32[]{:S(2)}) async-start(), calls=%async_computation | async-start | bytes 5242880 | tf_op jit(solution)/shard_map/all_gather | solution.py:177
  11.5 45.4 %collective-permute-start = (bf16[2048,256]{1,0:T(8,128)(2,1)S(1)}, bf16[2048,256]{1,0:T(8,128)(2,1)S(1)}, u32[]{:S(2)}, u32[]{:S(2)}) collective-permute-start(bf16[2048,256]{1,0:T(8,128)(2,1)S(1)} %pad_maximum_fusion.9), channel_id=1, source_target_pairs={{0,8},{2,10},{4,12},{6,14},{8,16},{10,18},{12,20},{14,22},{16,24},... | collective-permute-start | bytes 3145736 | tf_op jit(solution)/shard_map/ppermute | solution.py:175
  16.5 43.9 %copy-start.13 = (s32[4,3]{1,0:T(4,128)S(1)}, s32[4,3]{1,0:T(4,128)}, u32[]{:S(2)}) copy-start(s32[4,3]{1,0:T(4,128)} %param.8) | copy-start | bytes 148
  24.7 257.4 %collective-permute-start.12 = (bf16[2048,1024]{1,0:T(8,128)(2,1)}, bf16[2048,1024]{1,0:T(8,128)(2,1)}, u32[]{:S(2)}, u32[]{:S(2)}) collective-permute-start(bf16[2048,1024]{1,0:T(8,128)(2,1)} %get-tuple-element.72), channel_id=1, source_target_pairs={{0,1},{1,0},{2,3},{3,2},{4,5},{5,4},{6,7},{7,6},{8,9},{9,8},{10,11... | collective-permute-start | bytes 12582920 | tf_op jit(solution)/shard_map/ppermute | solution.py:162
  56.9 2.7 collective-permute-start.1
  59.6 164.5 %collective-permute-start.2 = (bf16[2048,256]{1,0:T(8,128)(2,1)}, bf16[2048,256]{1,0:T(8,128)(2,1)S(1)}, u32[]{:S(2)}, u32[]{:S(2)}) collective-permute-start(bf16[2048,256]{1,0:T(8,128)(2,1)} %collective-permute-done.1), channel_id=1, source_target_pairs={{16,24},{18,26},{20,28},{22,30},{17,25},{19,27},{21,29},{23,31}} | collective-permute-start | bytes 3145736 | tf_op jit(solution)/shard_map/ppermute | solution.py:175
  229.9 26.9 %collective-permute-start.11 = (bf16[4,512,256]{2,1,0:T(8,128)(2,1)}, bf16[4,512,256]{2,1,0:T(8,128)(2,1)}, u32[]{:S(2)}, u32[]{:S(2)}) collective-permute-start(bf16[4,512,256]{2,1,0:T(8,128)(2,1)} %get-tuple-element.54), channel_id=1, source_target_pairs={{0,6},{2,4},{4,2},{6,0},{8,14},{10,12},{12,10},{14,8},{16,22},{18,... | collective-permute-start | bytes 3145736 | tf_op jit(solution)/shard_map/ppermute | solution.py:206
  233.0 46.8 %collective-permute-start.10 = (bf16[4,512,256]{2,1,0:T(8,128)(2,1)}, bf16[4,512,256]{2,1,0:T(8,128)(2,1)}, u32[]{:S(2)}, u32[]{:S(2)}) collective-permute-start(bf16[4,512,256]{2,1,0:T(8,128)(2,1)} %get-tuple-element.53), channel_id=1, source_target_pairs={{0,4},{2,6},{4,0},{6,2},{8,12},{10,14},{12,8},{14,10},{16,20},{18,... | collective-permute-start | bytes 3145736 | tf_op jit(solution)/shard_map/ppermute | solution.py:206
  233.0 46.7 %collective-permute-start.9 = (bf16[4,512,256]{2,1,0:T(8,128)(2,1)}, bf16[4,512,256]{2,1,0:T(8,128)(2,1)}, u32[]{:S(2)}, u32[]{:S(2)}) collective-permute-start(bf16[4,512,256]{2,1,0:T(8,128)(2,1)} %get-tuple-element.52), channel_id=1, source_target_pairs={{0,2},{2,0},{4,6},{6,4},{8,10},{10,8},{12,14},{14,12},{16,18},{18,... | collective-permute-start | bytes 3145736 | tf_op jit(solution)/shard_map/ppermute | solution.py:206
  237.9 41.9 %copy-start.10 = (bf16[4,512,256]{2,1,0:T(8,128)(2,1)S(1)}, bf16[4,512,256]{2,1,0:T(8,128)(2,1)}, u32[]{:S(2)}) copy-start(bf16[4,512,256]{2,1,0:T(8,128)(2,1)} %get-tuple-element.51) | copy-start | bytes 3145732
  243.9 64.6 %collective-permute-start.5 = (bf16[4,512,256]{2,1,0:T(8,128)(2,1)}, bf16[4,512,256]{2,1,0:T(8,128)(2,1)S(1)}, u32[]{:S(2)}, u32[]{:S(2)}) collective-permute-start(bf16[4,512,256]{2,1,0:T(8,128)(2,1)} %get-tuple-element.44), channel_id=1, source_target_pairs={{0,6},{2,4},{4,2},{6,0},{8,14},{10,12},{12,10},{14,8},{16,22},{18,... | collective-permute-start | bytes 3145736 | tf_op jit(solution)/shard_map/ppermute | solution.py:206
  256.8 67.5 %collective-permute-start.4 = (bf16[4,512,256]{2,1,0:T(8,128)(2,1)}, bf16[4,512,256]{2,1,0:T(8,128)(2,1)S(1)}, u32[]{:S(2)}, u32[]{:S(2)}) collective-permute-start(bf16[4,512,256]{2,1,0:T(8,128)(2,1)} %get-tuple-element.43), channel_id=1, source_target_pairs={{0,4},{2,6},{4,0},{6,2},{8,12},{10,14},{12,8},{14,10},{16,20},{18,... | collective-permute-start | bytes 3145736 | tf_op jit(solution)/shard_map/ppermute | solution.py:206
  279.7 44.6 %collective-permute-start.3 = (bf16[4,512,256]{2,1,0:T(8,128)(2,1)}, bf16[4,512,256]{2,1,0:T(8,128)(2,1)S(1)}, u32[]{:S(2)}, u32[]{:S(2)}) collective-permute-start(bf16[4,512,256]{2,1,0:T(8,128)(2,1)} %get-tuple-element.42), channel_id=1, source_target_pairs={{0,2},{2,0},{4,6},{6,4},{8,10},{10,8},{12,14},{14,12},{16,18},{18,... | collective-permute-start | bytes 3145736 | tf_op jit(solution)/shard_map/ppermute | solution.py:206
  279.8 2.6 copy-start
  279.8 3.2 copy-start.3
  283.0 41.3 %copy-start.11 = (bf16[4,512,256]{2,1,0:T(8,128)(2,1)S(1)}, bf16[4,512,256]{2,1,0:T(8,128)(2,1)}, u32[]{:S(2)}) copy-start(bf16[4,512,256]{2,1,0:T(8,128)(2,1)} %get-tuple-element.41) | copy-start | bytes 3145732
  306.8 99.2 %collective-permute-start.13 = (bf16[2048,512]{1,0:T(8,128)(2,1)S(1)}, bf16[2048,512]{1,0:T(8,128)(2,1)}, u32[]{:S(2)}, u32[]{:S(2)}) collective-permute-start(bf16[2048,512]{1,0:T(8,128)(2,1)S(1)} %attend_head.6), channel_id=1, source_target_pairs={{0,1},{1,0},{2,3},{3,2},{4,5},{5,4},{6,7},{7,6},{8,9},{9,8},{10,11... | collective-permute-start | bytes 6291464 | tf_op jit(solution)/shard_map/ppermute | solution.py:216
  349.1 1.3 copy-start.6
  356.2 25.4 %collective-permute-start.8 = (bf16[4,512,256]{2,1,0:T(8,128)(2,1)}, bf16[4,512,256]{2,1,0:T(8,128)(2,1)S(1)}, u32[]{:S(2)}, u32[]{:S(2)}) collective-permute-start(bf16[4,512,256]{2,1,0:T(8,128)(2,1)} %get-tuple-element.49), channel_id=1, source_target_pairs={{0,6},{2,4},{4,2},{6,0},{8,14},{10,12},{12,10},{14,8},{16,22},{18,... | collective-permute-start | bytes 3145736 | tf_op jit(solution)/shard_map/ppermute | solution.py:206
  357.3 47.0 %collective-permute-start.7 = (bf16[4,512,256]{2,1,0:T(8,128)(2,1)}, bf16[4,512,256]{2,1,0:T(8,128)(2,1)S(1)}, u32[]{:S(2)}, u32[]{:S(2)}) collective-permute-start(bf16[4,512,256]{2,1,0:T(8,128)(2,1)} %get-tuple-element.48), channel_id=1, source_target_pairs={{0,4},{2,6},{4,0},{6,2},{8,12},{10,14},{12,8},{14,10},{16,20},{18,... | collective-permute-start | bytes 3145736 | tf_op jit(solution)/shard_map/ppermute | solution.py:206
  358.1 46.3 %collective-permute-start.6 = (bf16[4,512,256]{2,1,0:T(8,128)(2,1)}, bf16[4,512,256]{2,1,0:T(8,128)(2,1)S(1)}, u32[]{:S(2)}, u32[]{:S(2)}) collective-permute-start(bf16[4,512,256]{2,1,0:T(8,128)(2,1)} %get-tuple-element.47), channel_id=1, source_target_pairs={{0,2},{2,0},{4,6},{6,4},{8,10},{10,8},{12,14},{14,12},{16,18},{18,... | collective-permute-start | bytes 3145736 | tf_op jit(solution)/shard_map/ppermute | solution.py:206
  358.1 105.7 %collective-permute-start.17 = (bf16[2048,512]{1,0:T(8,128)(2,1)}, bf16[2048,512]{1,0:T(8,128)(2,1)}, u32[]{:S(2)}, u32[]{:S(2)}) collective-permute-start(bf16[2048,512]{1,0:T(8,128)(2,1)} %copy-done.6), channel_id=1, source_target_pairs={{0,1},{1,0},{2,3},{3,2},{4,5},{5,4},{6,7},{7,6},{8,9},{9,8},{10,11... | collective-permute-start | bytes 6291464 | tf_op jit(solution)/shard_map/ppermute | solution.py:216
  405.9 4.5 copy-start.9
  410.4 5.9 %copy-start.1 = (bf16[2048,512]{1,0:T(8,128)(2,1)S(1)}, bf16[2048,512]{1,0:T(8,128)(2,1)}, u32[]{:S(2)}) copy-start(bf16[2048,512]{1,0:T(8,128)(2,1)} %key_ref.9) | copy-start | bytes 6291460
  410.5 5.8 %copy-start.4 = (bf16[2048,512]{1,0:T(8,128)(2,1)S(1)}, bf16[2048,512]{1,0:T(8,128)(2,1)}, u32[]{:S(2)}) copy-start(bf16[2048,512]{1,0:T(8,128)(2,1)} %value_ref.9) | copy-start | bytes 6291460
  416.3 26.4 %copy-start.7 = (bf16[2048,512]{1,0:T(8,128)(2,1)S(1)}, bf16[2048,512]{1,0:T(8,128)(2,1)}, u32[]{:S(2)}) copy-start(bf16[2048,512]{1,0:T(8,128)(2,1)} %copy-done.6) | copy-start | bytes 6291460
  441.1 61.8 %collective-permute-start.18 = (bf16[2048,512]{1,0:T(8,128)(2,1)}, bf16[2048,512]{1,0:T(8,128)(2,1)S(1)}, u32[]{:S(2)}, u32[]{:S(2)}) collective-permute-start(bf16[2048,512]{1,0:T(8,128)(2,1)} %attend_head.7), channel_id=1, source_target_pairs={{0,1},{1,0},{2,3},{3,2},{4,5},{5,4},{6,7},{7,6},{8,9},{9,8},{10,11... | collective-permute-start | bytes 6291464 | tf_op jit(solution)/shard_map/ppermute | solution.py:216
  453.9 25.7 %collective-permute-start.16 = (bf16[4,512,256]{2,1,0:T(8,128)(2,1)}, bf16[4,512,256]{2,1,0:T(8,128)(2,1)S(1)}, u32[]{:S(2)}, u32[]{:S(2)}) collective-permute-start(bf16[4,512,256]{2,1,0:T(8,128)(2,1)} %get-tuple-element.63), channel_id=1, source_target_pairs={{0,6},{2,4},{4,2},{6,0},{8,14},{10,12},{12,10},{14,8},{16,22},{18,... | collective-permute-start | bytes 3145736 | tf_op jit(solution)/shard_map/ppermute | solution.py:206
  455.9 46.4 %collective-permute-start.15 = (bf16[4,512,256]{2,1,0:T(8,128)(2,1)}, bf16[4,512,256]{2,1,0:T(8,128)(2,1)S(1)}, u32[]{:S(2)}, u32[]{:S(2)}) collective-permute-start(bf16[4,512,256]{2,1,0:T(8,128)(2,1)} %get-tuple-element.62), channel_id=1, source_target_pairs={{0,4},{2,6},{4,0},{6,2},{8,12},{10,14},{12,8},{14,10},{16,20},{18,... | collective-permute-start | bytes 3145736 | tf_op jit(solution)/shard_map/ppermute | solution.py:206
  456.1 7.7 %copy-start.8 = (f32[2048,1024]{1,0:T(8,128)S(1)}, f32[2048,1024]{1,0:T(8,128)}, u32[]{:S(2)}) copy-start(f32[2048,1024]{1,0:T(8,128)} %fusion.7) | copy-start | bytes 25165828
  456.1 46.2 %collective-permute-start.14 = (bf16[4,512,256]{2,1,0:T(8,128)(2,1)}, bf16[4,512,256]{2,1,0:T(8,128)(2,1)S(1)}, u32[]{:S(2)}, u32[]{:S(2)}) collective-permute-start(bf16[4,512,256]{2,1,0:T(8,128)(2,1)} %get-tuple-element.61), channel_id=1, source_target_pairs={{0,2},{2,0},{4,6},{6,4},{8,10},{10,8},{12,14},{14,12},{16,18},{18,... | collective-permute-start | bytes 3145736 | tf_op jit(solution)/shard_map/ppermute | solution.py:206
  463.8 38.5 %copy-start.12 = (bf16[4,512,256]{2,1,0:T(8,128)(2,1)S(1)}, bf16[4,512,256]{2,1,0:T(8,128)(2,1)}, u32[]{:S(2)}) copy-start(bf16[4,512,256]{2,1,0:T(8,128)(2,1)} %get-tuple-element.60) | copy-start | bytes 3145732
  502.9 8.7 %copy-start.2 = (bf16[2048,512]{1,0:T(8,128)(2,1)S(1)}, bf16[2048,512]{1,0:T(8,128)(2,1)}, u32[]{:S(2)}) copy-start(bf16[2048,512]{1,0:T(8,128)(2,1)} %key_ref.9) | copy-start | bytes 6291460
  502.9 8.7 %copy-start.5 = (bf16[2048,512]{1,0:T(8,128)(2,1)S(1)}, bf16[2048,512]{1,0:T(8,128)(2,1)}, u32[]{:S(2)}) copy-start(bf16[2048,512]{1,0:T(8,128)(2,1)} %value_ref.9) | copy-start | bytes 6291460
  524.4 26.1 %collective-permute-start.20 = (bf16[1024,512]{1,0:T(8,128)(2,1)S(1)}, bf16[1024,512]{1,0:T(8,128)(2,1)S(1)}, u32[]{:S(2)}, u32[]{:S(2)}) collective-permute-start(bf16[1024,512]{1,0:T(8,128)(2,1)S(1)} %attend_head.9), channel_id=1, source_target_pairs={{0,1},{1,0},{2,3},{3,2},{4,5},{5,4},{6,7},{7,6},{8,9},{9,8},{10,11... | collective-permute-start | bytes 3145736 | tf_op jit(solution)/shard_map/ppermute | solution.py:216
  537.8 33.9 %collective-permute-start.19 = (bf16[1024,512]{1,0:T(8,128)(2,1)S(1)}, bf16[1024,512]{1,0:T(8,128)(2,1)S(1)}, u32[]{:S(2)}, u32[]{:S(2)}) collective-permute-start(bf16[1024,512]{1,0:T(8,128)(2,1)S(1)} %attend_head.8), channel_id=1, source_target_pairs={{0,1},{1,0},{2,3},{3,2},{4,5},{5,4},{6,7},{7,6},{8,9},{9,8},{10,11... | collective-permute-start | bytes 3145736 | tf_op jit(solution)/shard_map/ppermute | solution.py:216
Sparse Core Ops, SparseCore 0:
  10.3 96.3 all-gather.11
  108.3 96.2 all-gather.9
  206.2 100.8 all-gather.7

commit v4 on v3

--- a/solution.py
+++ b/solution.py
@@ -161,6 +161,7 @@
         share = lax.dynamic_slice_in_dim(out_weight, start, out_columns, axis=1)
         weights.append(share if s == 0 else lax.ppermute(share, "head", turns[s]))
 
+    everyone = lax.all_gather(selected, "ctx", axis=0, tiled=True).reshape(ctx_count, request_count)
     owners = ctx_count // MATES
     columns = [[z * MATES + q for z in range(owners)] for q in range(MATES)]
     chained = kv_heads - 1 if kv_heads > 2 else None
@@ -169,6 +170,7 @@
         lanes = slice(head * HEAD_SIZE, (head + 1) * HEAD_SIZE)
         pair = jnp.concatenate([keys[:, lanes], values[:, lanes]], axis=1)
         if head == chained:
+            pair, everyone = lax.optimization_barrier((pair, everyone))
             chain = [pair]
             for s in range(1, owners):
                 up = [(i, i + MATES) for i in range((s - 1) * MATES, ctx_count - MATES)]
@@ -176,11 +178,10 @@
         else:
             gathered[head] = lax.all_gather(pair, "ctx", axis_index_groups=columns, axis=0)
     if chained is not None:
-        gathered[0], *chain = lax.optimization_barrier((gathered[0], *chain))
+        gathered[0], *chain[:-1] = lax.optimization_barrier((gathered[0], *chain[:-1]))
         gathered[chained] = jnp.stack(chain, axis=0)
 
     wanted = selected.reshape(request_count)
-    everyone = lax.all_gather(selected, "ctx", axis=0, tiled=True).reshape(ctx_count, request_count)
     mine = ctx_index % MATES
     mates = jnp.bitwise_xor(ctx_index, jnp.arange(MATES))
     asked = everyone[mates][:, None, :]
@@ -224,25 +225,29 @@
         order = [0, chained] + list(range(1, chained))
     last = order[-1]
     fetched = {order[0]: fetch(order[0], None)}
-    if chained is not None:
-        fetched[chained] = fetch(chained, None)
     total = None
     pending = []
-    previous = None
-    for head in order[:-1]:
-        if head not in fetched:
-            fetched[head] = fetch(head, previous)
-        arrived = jnp.concatenate(fetched[head], axis=0)
-        if previous is None:
+    done = []
+    for step, head in enumerate(order[:-1]):
+        parts = fetched[head]
+        if head == chained:
+            following = order[step + 1]
+            fetched[following] = fetch(following, done[0])
+            parts[0], fetched[following][0] = lax.optimization_barrier(
+                (parts[0], fetched[following][0])
+            )
+        arrived = jnp.concatenate(parts, axis=0)
+        if not done:
             arrived, *weights = lax.optimization_barrier((arrived, *weights))
         elif len(pending) > 1:
             total = project(total, pending[0][1], weights, pending[0][0])
             pending = pending[1:]
             arrived, total = lax.optimization_barrier((arrived, total))
-        previous = attend(head, arrived, 0, blk_dev)
-        pending.append((head, spread(previous)))
-    if last not in fetched:
-        fetched[last] = fetch(last, previous)
+        done.append(attend(head, arrived, 0, blk_dev))
+        following = order[step + 1]
+        if following not in fetched:
+            fetched[following] = fetch(following, done[-1])
+        pending.append((head, spread(done[-1])))
     arrived = jnp.concatenate(fetched[last], axis=0)
     for head, part in pending:
         total = project(total, part, weights, head)

time: 592 us -> 545 us (0.921)
  the two profiles are of different devices: /device:TPU:0 before, /device:TPU:17 now
where the time goes in v4:
time: 545 us; the launch traced here: 536 us
  waiting for transfers between devices  274 us (50%)
  Pallas kernels  122 us (22%)
  matrix products  48.8 us (9%)
  starting transfers between devices  30.3 us (6%)
  blocking collectives  17.8 us (3%)
  other arithmetic  16 us (3%)
  between operations  13.9 us (3%)
  local copies, waits for them, and re-layouts  13.6 us (2%)
    ppermute x3, waiting for transfers between devices, per_device(): chain.append(lax.ppermute(chain[-1], 'ctx', up))  160 us
    pallas_call x5, Pallas kernels, attend_head(): pl.pallas_call(functools.partial(attention_kernel, first, group), grid_sp...  98.4 us
    ppermute x12, waiting for transfers between devices, fetch(): lax.ppermute(packed[k], 'ctx', hops[k])  88.2 us
    dot_general x10, matrix products, project(): term = jnp.dot(part, weight[rows], preferred_element_type=jnp.float32)  48.8 us
    ppermute x5, waiting for transfers between devices, spread(): lax.ppermute(attended, 'head', turns[s])  25.6 us
    pallas_call x4, Pallas kernels, pack_head(): pl.pallas_call(pack_kernel, grid_spec=pltpu.PrefetchScalarGridSpec(num_sc...  23.8 us
    all_gather x1, blocking collectives, per_device(): lax.all_gather(selected, 'ctx', axis=0, tiled=True)  17.8 us
    ppermute x12, starting transfers between devices, fetch(): lax.ppermute(packed[k], 'ctx', hops[k])  16.4 us
  transfers between devices with their start and end apart: 24, of which 11 were waited for; matrix products, arithmetic and copies ran while one was open for 11% of the time, Pallas kernels for 20%

profile of v4, /device:TPU:17, one launch (start us, length us, event | category | flops | bytes accessed | tf_op | source)
XLA Modules:
  0.0 536.3 jit_solution(2092228097841485597)
XLA Ops:
  6.5 2.6 fusion.32
  9.1 1.1 pad_maximum_fusion.8
  10.3 1.1 pad_maximum_fusion.9
  11.5 7.8 %constant_dynamic-slice_fusion = (bf16[2048,1024]{1,0:T(8,128)(2,1)}, bf16[2048,1024]{1,0:T(8,128)(2,1)}) fusion(bf16[2048,2048]{1,0:T(8,128)(2,1)} %param.9, s32[]{:T(128)S(6)} %select_n.96, s32[]{:T(128)S(6)} %select_n.95), kind=kLoop, calls=%fused_computation.78 | loop fusion | bytes 16777224 | tf_op jit(solution)/shard_map/dynamic_slice | solution.py:161
  19.3 1.2 collective-permute-start.6
  20.5 17.8 %all-gather.3 = s32[16,4,3]{2,1,0:T(4,128)S(1)} all-gather(s32[1,4,3]{2,1,0:T(4,128)S(1)} %bitcast.39), channel_id=1, replica_groups=mesh['ctx'=16,'head'=2] {'ctx'}, dimensions={0}, use_global_device_ids=true | all-gather | bytes 816 | tf_op jit(solution)/shard_map/all_gather | solution.py:164
  38.5 0.1 pad_maximum_fusion.6
  38.6 5.6 %collective-permute-start = (bf16[2048,256]{1,0:T(8,128)(2,1)S(1)}, bf16[2048,256]{1,0:T(8,128)(2,1)S(1)}, u32[]{:S(2)}, u32[]{:S(2)}) collective-permute-start(bf16[2048,256]{1,0:T(8,128)(2,1)S(1)} %pad_maximum_fusion.6), channel_id=1, source_target_pairs={{0,8},{2,10},{4,12},{6,14},{8,16},{10,18},{12,20},{14,22},{16,24},... | collective-permute-start | bytes 3145736 | tf_op jit(solution)/shard_map/ppermute | solution.py:177
  44.2 67.2 %collective-permute-done = bf16[2048,256]{1,0:T(8,128)(2,1)S(1)} collective-permute-done((bf16[2048,256]{1,0:T(8,128)(2,1)S(1)}, bf16[2048,256]{1,0:T(8,128)(2,1)S(1)}, u32[]{:S(2)}, u32[]{:S(2)}) %collective-permute-start) | collective-permute-done | bytes 1048608 | tf_op jit(solution)/shard_map/ppermute | solution.py:177
  111.4 3.1 collective-permute-start.1
  114.6 0.6 gather_fusion
  115.2 60.3 %collective-permute-done.1 = bf16[2048,256]{1,0:T(8,128)(2,1)} collective-permute-done((bf16[2048,256]{1,0:T(8,128)(2,1)S(1)}, bf16[2048,256]{1,0:T(8,128)(2,1)}, u32[]{:S(2)}, u32[]{:S(2)}) %collective-permute-start.1) | collective-permute-done | bytes 1048608 | tf_op jit(solution)/shard_map/ppermute | solution.py:177
  175.4 2.3 collective-permute-start.2
  177.7 0.2 select_reduce_fusion
  178.2 0.6 compare_select_fusion.8.block_ref
  178.8 5.8 %pack_head.4 = (bf16[4,512,256]{2,1,0:T(8,128)(2,1)}, bf16[4,512,256]{2,1,0:T(8,128)(2,1)}, bf16[4,512,256]{2,1,0:T(8,128)(2,1)}, bf16[4,512,256]{2,1,0:T(8,128)(2,1)}) custom-call(s32[16]{0:T(128)} %compare_select_fusion.8.block_ref, bf16[4,2048,256]{2,1,0:T(8,128)(2,1)} %bitcast.27, bf16[4,2048,256]{2,1,0:T(8,128)(2,1)} %bitcast.28, ...), custom_call_target="tpu_custom_call" | custom-call | bytes 8388608 | tf_op jit(solution)/shard_map/pack_head/pallas_call | solution.py:34
  184.6 1.8 collective-permute-start.5
  186.3 6.1 %collective-permute-start.4 = (bf16[4,512,256]{2,1,0:T(8,128)(2,1)}, bf16[4,512,256]{2,1,0:T(8,128)(2,1)}, u32[]{:S(2)}, u32[]{:S(2)}) collective-permute-start(bf16[4,512,256]{2,1,0:T(8,128)(2,1)} %get-tuple-element.49), channel_id=1, source_target_pairs={{0,4},{2,6},{4,0},{6,2},{8,12},{10,14},{12,8},{14,10},{16,20},{18,... | collective-permute-start | bytes 3145736 | tf_op jit(solution)/shard_map/ppermute | solution.py:207
  192.5 0.6 gather_fusion.1
  193.0 0.1 copy.22
  193.1 0.6 reshape.109.block_ref
  193.8 32.3 %collective-permute-done.2 = bf16[2048,256]{1,0:T(8,128)(2,1)} collective-permute-done((bf16[2048,256]{1,0:T(8,128)(2,1)}, bf16[2048,256]{1,0:T(8,128)(2,1)}, u32[]{:S(2)}, u32[]{:S(2)}) %collective-permute-start.2) | collective-permute-done | bytes 1048608 | tf_op jit(solution)/shard_map/ppermute | solution.py:177
  226.1 3.6 pad_maximum_fusion.refs_0_.refs_1_.refs_2_.refs_3_
  229.7 3.2 collective-permute-done.4
  232.9 2.3 pad_maximum_fusion.1.far0.far1.far2
  235.2 0.2 copy-done
  235.4 0.6 copy-done.3
  236.0 23.8 %attend_head.5 = bf16[2048,512]{1,0:T(8,128)(2,1)S(1)} custom-call(s32[12]{0:T(128)S(1)} %add.119.source_ref, s32[12]{0:T(128)S(1)} %compare_convert_fusion.live_ref, bf16[2048,2048]{1,0:T(8,128)(2,1)} %query_ref.9, bf16[2048,512]{1,0:T(8,128)(2,1)S(1)} %copy-done, bf16[2048,512]{1,0:T(8,128)(2,1)S(1)} %copy-done.3, ...), custom_call_target="tpu_custom_call" | custom-call | flops 17179869184 | bytes 8388608 | tf_op jit(solution)/shard_map/attend_head/pallas_call | solution.py:119
  259.8 6.1 %pack_head.5 = (bf16[4,512,256]{2,1,0:T(8,128)(2,1)}, bf16[4,512,256]{2,1,0:T(8,128)(2,1)}, bf16[4,512,256]{2,1,0:T(8,128)(2,1)}, bf16[4,512,256]{2,1,0:T(8,128)(2,1)}) custom-call(s32[16]{0:T(128)} %reshape.109.block_ref, bf16[4,2048,256]{2,1,0:T(8,128)(2,1)} %pad_maximum_fusion.refs_0_.refs_1_.refs_2_.refs_3_, ...), custom_call_target="tpu_custom_call" | custom-call | bytes 8388608 | tf_op jit(solution)/shard_map/pack_head/pallas_call | solution.py:34
  265.9 1.7 collective-permute-start.16
  267.7 0.5 collective-permute-start.14
  268.2 1.1 pad_maximum_fusion.7
  269.4 6.1 %pack_head.6 = (bf16[4,512,256]{2,1,0:T(8,128)(2,1)}, bf16[4,512,256]{2,1,0:T(8,128)(2,1)}, bf16[4,512,256]{2,1,0:T(8,128)(2,1)}, bf16[4,512,256]{2,1,0:T(8,128)(2,1)}) custom-call(s32[16]{0:T(128)} %compare_select_fusion.8.block_ref, bf16[4,2048,256]{2,1,0:T(8,128)(2,1)} %bitcast.23, bf16[4,2048,256]{2,1,0:T(8,128)(2,1)} %bitcast.24, ...), custom_call_target="tpu_custom_call" | custom-call | bytes 8388608 | tf_op jit(solution)/shard_map/pack_head/pallas_call | solution.py:34
  275.5 1.9 collective-permute-start.9
  277.3 14.7 %collective-permute-done.16 = bf16[4,512,256]{2,1,0:T(8,128)(2,1)} collective-permute-done((bf16[4,512,256]{2,1,0:T(8,128)(2,1)}, bf16[4,512,256]{2,1,0:T(8,128)(2,1)}, u32[]{:S(2)}, u32[]{:S(2)}) %collective-permute-start.16) | collective-permute-done | bytes 1048608 | tf_op jit(solution)/shard_map/ppermute | solution.py:207
  292.1 21.5 %collective-permute-done.15 = bf16[4,512,256]{2,1,0:T(8,128)(2,1)} collective-permute-done((bf16[4,512,256]{2,1,0:T(8,128)(2,1)}, bf16[4,512,256]{2,1,0:T(8,128)(2,1)}, u32[]{:S(2)}, u32[]{:S(2)}) %collective-permute-start.15) | collective-permute-done | bytes 1048608 | tf_op jit(solution)/shard_map/ppermute | solution.py:207
  313.5 1.4 collective-permute-start.7
  314.9 2.1 pad_maximum_fusion.4.far0.far1.far2
  317.1 25.1 %attend_head.7 = bf16[2048,512]{1,0:T(8,128)(2,1)} custom-call(s32[12]{0:T(128)S(1)} %get-tuple-element.77.source_ref, s32[12]{0:T(128)S(1)} %compare_convert_fusion.live_ref, bf16[2048,2048]{1,0:T(8,128)(2,1)} %query_ref.9, bf16[2048,512]{1,0:T(8,128)(2,1)S(1)} %copy-done.1, bf16[2048,512]{1,0:T(8,128)(2,1)S(1)} %copy-done.4, ...), custom_call_target="tpu_custom_call" | custom-call | flops 17179869184 | bytes 8388608 | tf_op jit(solution)/shard_map/attend_head/pallas_call | solution.py:119
  342.2 14.7 %collective-permute-done.8 = bf16[4,512,256]{2,1,0:T(8,128)(2,1)S(1)} collective-permute-done((bf16[4,512,256]{2,1,0:T(8,128)(2,1)}, bf16[4,512,256]{2,1,0:T(8,128)(2,1)S(1)}, u32[]{:S(2)}, u32[]{:S(2)}) %collective-permute-start.8) | collective-permute-done | bytes 1048608 | tf_op jit(solution)/shard_map/ppermute | solution.py:207
  356.9 0.5 pad_maximum_fusion.2.far0.far1.far2
  357.5 4.3 fusion.9
  361.8 7.1 %convolution_add_fusion = f32[2048,1024]{1,0:T(8,128)} fusion(f32[2048,1024]{1,0:T(8,128)S(1)} %fusion.9, bf16[2048,512]{1,0:T(8,128)(2,1)S(1)} %attend_head.5, bf16[2048,1024]{1,0:T(8,128)(2,1)} %get-tuple-element.60), kind=kOutput, calls=%fused_computation.12 | convolution fusion | flops 2149580800 | bytes 19922944 | tf_op jit(solution)/shard_map/dot_general | solution.py:212
  368.9 24.0 %attend_head.6 = bf16[2048,512]{1,0:T(8,128)(2,1)S(1)} custom-call(s32[12]{0:T(128)S(1)} %add.119.source_ref, s32[12]{0:T(128)S(1)} %compare_convert_fusion.live_ref, bf16[2048,2048]{1,0:T(8,128)(2,1)} %query_ref.9, bf16[2048,512]{1,0:T(8,128)(2,1)S(1)} %copy-done.1, bf16[2048,512]{1,0:T(8,128)(2,1)S(1)} %copy-done.4, ...), custom_call_target="tpu_custom_call" | custom-call | flops 17179869184 | bytes 8388608 | tf_op jit(solution)/shard_map/attend_head/pallas_call | solution.py:119
  392.9 5.8 %pack_head.7 = (bf16[4,512,256]{2,1,0:T(8,128)(2,1)}, bf16[4,512,256]{2,1,0:T(8,128)(2,1)}, bf16[4,512,256]{2,1,0:T(8,128)(2,1)}, bf16[4,512,256]{2,1,0:T(8,128)(2,1)}) custom-call(s32[16]{0:T(128)} %compare_select_fusion.8.block_ref, bf16[4,2048,256]{2,1,0:T(8,128)(2,1)} %bitcast.31, bf16[4,2048,256]{2,1,0:T(8,128)(2,1)} %bitcast.32, ...), custom_call_target="tpu_custom_call" | custom-call | bytes 8388608 | tf_op jit(solution)/shard_map/pack_head/pallas_call | solution.py:34
  398.7 1.3 collective-permute-start.13
  400.0 1.7 collective-permute-start.12
  401.7 4.3 fusion.7
  406.0 7.0 %fusion.1 = f32[2048,1024]{1,0:T(8,128)} fusion(bf16[2048,512]{1,0:T(8,128)(2,1)S(1)} %attend_head.6, bf16[2048,1024]{1,0:T(8,128)(2,1)} %get-tuple-element.60), kind=kOutput, calls=%fused_computation.18 | convolution fusion | flops 2147483648 | bytes 11534336 | tf_op jit(solution)/shard_map/dot_general | solution.py:212
  413.0 10.7 %collective-permute-done.13 = bf16[4,512,256]{2,1,0:T(8,128)(2,1)S(1)} collective-permute-done((bf16[4,512,256]{2,1,0:T(8,128)(2,1)}, bf16[4,512,256]{2,1,0:T(8,128)(2,1)S(1)}, u32[]{:S(2)}, u32[]{:S(2)}) %collective-permute-start.13) | collective-permute-done | bytes 1048608 | tf_op jit(solution)/shard_map/ppermute | solution.py:207
  423.7 23.4 %collective-permute-done.12 = bf16[4,512,256]{2,1,0:T(8,128)(2,1)S(1)} collective-permute-done((bf16[4,512,256]{2,1,0:T(8,128)(2,1)}, bf16[4,512,256]{2,1,0:T(8,128)(2,1)S(1)}, u32[]{:S(2)}, u32[]{:S(2)}) %collective-permute-start.12) | collective-permute-done | bytes 1048608 | tf_op jit(solution)/shard_map/ppermute | solution.py:207
  447.1 0.8 pad_maximum_fusion.3.far0.far1.far2
  447.9 7.6 %add_add_fusion.1 = f32[2048,1024]{1,0:T(8,128)} fusion(f32[2048,1024]{1,0:T(8,128)S(1)} %bitcast.36, f32[2048,1024]{1,0:T(8,128)S(1)} %fusion.7, bf16[2048,512]{1,0:T(8,128)(2,1)} %collective-permute-done.17, bf16[2048,1024]{1,0:T(8,128)(2,1)} %collective-permute-done.6), kind=kOutput, calls=%fused_computation.3 | convolution fusion | flops 2151677952 | bytes 28311552 | tf_op jit(solution)/shard_map/dot_general | solution.py:212
  455.5 8.6 %add_add_fusion = f32[2048,1024]{1,0:T(8,128)S(1)} fusion(f32[2048,1024]{1,0:T(8,128)} %add_add_fusion.1, f32[2048,1024]{1,0:T(8,128)} %fusion.1, bf16[2048,512]{1,0:T(8,128)(2,1)S(1)} %collective-permute-done.18, bf16[2048,1024]{1,0:T(8,128)(2,1)} %collective-permute-done.6), kind=kOutput, calls=%fused_computation.2 | convolution fusion | flops 2151677952 | bytes 28311552 | tf_op jit(solution)/shard_map/dot_general | solution.py:212
  464.2 12.7 %attend_head.9 = bf16[1024,512]{1,0:T(8,128)(2,1)S(1)} custom-call(s32[12]{0:T(128)S(1)} %add.119.source_ref, s32[12]{0:T(128)S(1)} %compare_convert_fusion.live_ref, bf16[2048,2048]{1,0:T(8,128)(2,1)} %query_ref.9, bf16[2048,512]{1,0:T(8,128)(2,1)S(1)} %copy-done.2, bf16[2048,512]{1,0:T(8,128)(2,1)S(1)} %copy-done.5, ...), custom_call_target="tpu_custom_call" | custom-call | flops 8589934592 | bytes 4194304 | tf_op jit(solution)/shard_map/attend_head/pallas_call | solution.py:119
  476.9 12.9 %attend_head.8 = bf16[1024,512]{1,0:T(8,128)(2,1)S(1)} custom-call(s32[12]{0:T(128)S(1)} %add.119.source_ref, s32[12]{0:T(128)S(1)} %compare_convert_fusion.live_ref, bf16[2048,2048]{1,0:T(8,128)(2,1)} %query_ref.9, bf16[2048,512]{1,0:T(8,128)(2,1)S(1)} %copy-done.2, bf16[2048,512]{1,0:T(8,128)(2,1)S(1)} %copy-done.5, ...), custom_call_target="tpu_custom_call" | custom-call | flops 8589934592 | bytes 4194304 | tf_op jit(solution)/shard_map/attend_head/pallas_call | solution.py:119
  489.9 1.5 collective-permute-start.19
  491.4 2.5 fusion.14
  493.9 2.5 fusion.16
  496.3 5.8 %collective-permute-done.20 = bf16[1024,512]{1,0:T(8,128)(2,1)S(1)} collective-permute-done((bf16[1024,512]{1,0:T(8,128)(2,1)S(1)}, bf16[1024,512]{1,0:T(8,128)(2,1)S(1)}, u32[]{:S(2)}, u32[]{:S(2)}) %collective-permute-start.20) | collective-permute-done | bytes 1048608 | tf_op jit(solution)/shard_map/ppermute | solution.py:217
  502.1 2.5 add_convert_fusion
  504.6 19.9 %collective-permute-done.19 = bf16[1024,512]{1,0:T(8,128)(2,1)S(1)} collective-permute-done((bf16[1024,512]{1,0:T(8,128)(2,1)S(1)}, bf16[1024,512]{1,0:T(8,128)(2,1)S(1)}, u32[]{:S(2)}, u32[]{:S(2)}) %collective-permute-start.19) | collective-permute-done | bytes 1048608 | tf_op jit(solution)/shard_map/ppermute | solution.py:217
  524.4 2.5 add_convert_fusion.1
  526.9 2.5 pad_maximum_fusion.5
  (67 shorter events, 1.0 us)
Async XLA Ops:
  6.5 172.3 %all-gather.10.cloned.1.call-start = ((), (), s32[]{:S(2)}) async-start(), calls=%async_computation.1 | async-start | bytes 5242880 | tf_op jit(solution)/shard_map/all_gather | solution.py:179
  10.2 259.1 %all-gather.12.cloned.1.call-start = ((), (), s32[]{:S(2)}) async-start(), calls=%async_computation.2 | async-start | bytes 5242880 | tf_op jit(solution)/shard_map/all_gather | solution.py:179
  11.4 381.5 %all-gather.8.cloned.1.call-start = ((), (), s32[]{:S(2)}) async-start(), calls=%async_computation | async-start | bytes 5242880 | tf_op jit(solution)/shard_map/all_gather | solution.py:179
  11.5 9.0 %copy-start.10 = (s32[4,3]{1,0:T(4,128)S(1)}, s32[4,3]{1,0:T(4,128)}, u32[]{:S(2)}) copy-start(s32[4,3]{1,0:T(4,128)} %param.8) | copy-start | bytes 148
  19.3 215.9 %collective-permute-start.6 = (bf16[2048,1024]{1,0:T(8,128)(2,1)}, bf16[2048,1024]{1,0:T(8,128)(2,1)}, u32[]{:S(2)}, u32[]{:S(2)}) collective-permute-start(bf16[2048,1024]{1,0:T(8,128)(2,1)} %get-tuple-element.80), channel_id=1, source_target_pairs={{0,1},{1,0},{2,3},{3,2},{4,5},{5,4},{6,7},{7,6},{8,9},{9,8},{10,11... | collective-permute-start | bytes 12582920 | tf_op jit(solution)/shard_map/ppermute | solution.py:162
  38.6 72.8 %collective-permute-start = (bf16[2048,256]{1,0:T(8,128)(2,1)S(1)}, bf16[2048,256]{1,0:T(8,128)(2,1)S(1)}, u32[]{:S(2)}, u32[]{:S(2)}) collective-permute-start(bf16[2048,256]{1,0:T(8,128)(2,1)S(1)} %pad_maximum_fusion.6), channel_id=1, source_target_pairs={{0,8},{2,10},{4,12},{6,14},{8,16},{10,18},{12,20},{14,22},{16,24},... | collective-permute-start | bytes 3145736 | tf_op jit(solution)/shard_map/ppermute | solution.py:177
  111.4 64.0 %collective-permute-start.1 = (bf16[2048,256]{1,0:T(8,128)(2,1)S(1)}, bf16[2048,256]{1,0:T(8,128)(2,1)}, u32[]{:S(2)}, u32[]{:S(2)}) collective-permute-start(bf16[2048,256]{1,0:T(8,128)(2,1)S(1)} %collective-permute-done), channel_id=1, source_target_pairs={{8,16},{10,18},{12,20},{14,22},{16,24},{18,26},{20,28},{22,30},{9,... | collective-permute-start | bytes 3145736 | tf_op jit(solution)/shard_map/ppermute | solution.py:177
  175.4 50.7 %collective-permute-start.2 = (bf16[2048,256]{1,0:T(8,128)(2,1)}, bf16[2048,256]{1,0:T(8,128)(2,1)}, u32[]{:S(2)}, u32[]{:S(2)}) collective-permute-start(bf16[2048,256]{1,0:T(8,128)(2,1)} %collective-permute-done.1), channel_id=1, source_target_pairs={{16,24},{18,26},{20,28},{22,30},{17,25},{19,27},{21,29},{23,31}} | collective-permute-start | bytes 3145736 | tf_op jit(solution)/shard_map/ppermute | solution.py:177
  184.6 45.1 %collective-permute-start.5 = (bf16[4,512,256]{2,1,0:T(8,128)(2,1)}, bf16[4,512,256]{2,1,0:T(8,128)(2,1)}, u32[]{:S(2)}, u32[]{:S(2)}) collective-permute-start(bf16[4,512,256]{2,1,0:T(8,128)(2,1)} %get-tuple-element.50), channel_id=1, source_target_pairs={{0,6},{2,4},{4,2},{6,0},{8,14},{10,12},{12,10},{14,8},{16,22},{18,... | collective-permute-start | bytes 3145736 | tf_op jit(solution)/shard_map/ppermute | solution.py:207
  186.3 46.5 %collective-permute-start.4 = (bf16[4,512,256]{2,1,0:T(8,128)(2,1)}, bf16[4,512,256]{2,1,0:T(8,128)(2,1)}, u32[]{:S(2)}, u32[]{:S(2)}) collective-permute-start(bf16[4,512,256]{2,1,0:T(8,128)(2,1)} %get-tuple-element.49), channel_id=1, source_target_pairs={{0,4},{2,6},{4,0},{6,2},{8,12},{10,14},{12,8},{14,10},{16,20},{18,... | collective-permute-start | bytes 3145736 | tf_op jit(solution)/shard_map/ppermute | solution.py:207
  192.5 40.4 %collective-permute-start.3 = (bf16[4,512,256]{2,1,0:T(8,128)(2,1)}, bf16[4,512,256]{2,1,0:T(8,128)(2,1)}, u32[]{:S(2)}, u32[]{:S(2)}) collective-permute-start(bf16[4,512,256]{2,1,0:T(8,128)(2,1)} %get-tuple-element.48), channel_id=1, source_target_pairs={{0,2},{2,0},{4,6},{6,4},{8,10},{10,8},{12,14},{14,12},{16,18},{18,... | collective-permute-start | bytes 3145736 | tf_op jit(solution)/shard_map/ppermute | solution.py:207
  226.1 6.7 %copy-start.7 = (bf16[4,512,256]{2,1,0:T(8,128)(2,1)S(1)}, bf16[4,512,256]{2,1,0:T(8,128)(2,1)}, u32[]{:S(2)}) copy-start(bf16[4,512,256]{2,1,0:T(8,128)(2,1)} %get-tuple-element.47) | copy-start | bytes 3145732
  232.8 2.5 copy-start
  232.9 3.2 copy-start.3
  265.9 26.1 %collective-permute-start.16 = (bf16[4,512,256]{2,1,0:T(8,128)(2,1)}, bf16[4,512,256]{2,1,0:T(8,128)(2,1)}, u32[]{:S(2)}, u32[]{:S(2)}) collective-permute-start(bf16[4,512,256]{2,1,0:T(8,128)(2,1)} %get-tuple-element.72), channel_id=1, source_target_pairs={{0,6},{2,4},{4,2},{6,0},{8,14},{10,12},{12,10},{14,8},{16,22},{18,... | collective-permute-start | bytes 3145736 | tf_op jit(solution)/shard_map/ppermute | solution.py:207
  267.7 45.8 %collective-permute-start.15 = (bf16[4,512,256]{2,1,0:T(8,128)(2,1)}, bf16[4,512,256]{2,1,0:T(8,128)(2,1)}, u32[]{:S(2)}, u32[]{:S(2)}) collective-permute-start(bf16[4,512,256]{2,1,0:T(8,128)(2,1)} %get-tuple-element.71), channel_id=1, source_target_pairs={{0,4},{2,6},{4,0},{6,2},{8,12},{10,14},{12,8},{14,10},{16,20},{18,... | collective-permute-start | bytes 3145736 | tf_op jit(solution)/shard_map/ppermute | solution.py:207
  267.7 47.2 %collective-permute-start.14 = (bf16[4,512,256]{2,1,0:T(8,128)(2,1)}, bf16[4,512,256]{2,1,0:T(8,128)(2,1)}, u32[]{:S(2)}, u32[]{:S(2)}) collective-permute-start(bf16[4,512,256]{2,1,0:T(8,128)(2,1)} %get-tuple-element.70), channel_id=1, source_target_pairs={{0,2},{2,0},{4,6},{6,4},{8,10},{10,8},{12,14},{14,12},{16,18},{18,... | collective-permute-start | bytes 3145736 | tf_op jit(solution)/shard_map/ppermute | solution.py:207
  269.3 88.2 %collective-permute-start.10 = (bf16[2048,512]{1,0:T(8,128)(2,1)S(1)}, bf16[2048,512]{1,0:T(8,128)(2,1)}, u32[]{:S(2)}, u32[]{:S(2)}) collective-permute-start(bf16[2048,512]{1,0:T(8,128)(2,1)S(1)} %attend_head.5), channel_id=1, source_target_pairs={{0,1},{1,0},{2,3},{3,2},{4,5},{5,4},{6,7},{7,6},{8,9},{9,8},{10,11... | collective-permute-start | bytes 6291464 | tf_op jit(solution)/shard_map/ppermute | solution.py:217
  269.4 45.5 %copy-start.6 = (bf16[4,512,256]{2,1,0:T(8,128)(2,1)S(1)}, bf16[4,512,256]{2,1,0:T(8,128)(2,1)}, u32[]{:S(2)}) copy-start(bf16[4,512,256]{2,1,0:T(8,128)(2,1)} %get-tuple-element.69) | copy-start | bytes 3145732
  275.5 66.7 %collective-permute-start.9 = (bf16[4,512,256]{2,1,0:T(8,128)(2,1)}, bf16[4,512,256]{2,1,0:T(8,128)(2,1)S(1)}, u32[]{:S(2)}, u32[]{:S(2)}) collective-permute-start(bf16[4,512,256]{2,1,0:T(8,128)(2,1)} %get-tuple-element.59), channel_id=1, source_target_pairs={{0,6},{2,4},{4,2},{6,0},{8,14},{10,12},{12,10},{14,8},{16,22},{18,... | collective-permute-start | bytes 3145736 | tf_op jit(solution)/shard_map/ppermute | solution.py:207
  292.1 64.9 %collective-permute-start.8 = (bf16[4,512,256]{2,1,0:T(8,128)(2,1)}, bf16[4,512,256]{2,1,0:T(8,128)(2,1)S(1)}, u32[]{:S(2)}, u32[]{:S(2)}) collective-permute-start(bf16[4,512,256]{2,1,0:T(8,128)(2,1)} %get-tuple-element.58), channel_id=1, source_target_pairs={{0,4},{2,6},{4,0},{6,2},{8,12},{10,14},{12,8},{14,10},{16,20},{18,... | collective-permute-start | bytes 3145736 | tf_op jit(solution)/shard_map/ppermute | solution.py:207
  313.5 3.6 copy-start.1
  313.5 3.6 copy-start.4
  313.5 43.4 %collective-permute-start.7 = (bf16[4,512,256]{2,1,0:T(8,128)(2,1)}, bf16[4,512,256]{2,1,0:T(8,128)(2,1)S(1)}, u32[]{:S(2)}, u32[]{:S(2)}) collective-permute-start(bf16[4,512,256]{2,1,0:T(8,128)(2,1)} %get-tuple-element.57), channel_id=1, source_target_pairs={{0,2},{2,0},{4,6},{6,4},{8,10},{10,8},{12,14},{14,12},{16,18},{18,... | collective-permute-start | bytes 3145736 | tf_op jit(solution)/shard_map/ppermute | solution.py:207
  317.1 39.8 %copy-start.8 = (bf16[4,512,256]{2,1,0:T(8,128)(2,1)S(1)}, bf16[4,512,256]{2,1,0:T(8,128)(2,1)}, u32[]{:S(2)}) copy-start(bf16[4,512,256]{2,1,0:T(8,128)(2,1)} %get-tuple-element.56) | copy-start | bytes 3145732
  342.2 105.7 %collective-permute-start.17 = (bf16[2048,512]{1,0:T(8,128)(2,1)}, bf16[2048,512]{1,0:T(8,128)(2,1)}, u32[]{:S(2)}, u32[]{:S(2)}) collective-permute-start(bf16[2048,512]{1,0:T(8,128)(2,1)} %attend_head.7), channel_id=1, source_target_pairs={{0,1},{1,0},{2,3},{3,2},{4,5},{5,4},{6,7},{7,6},{8,9},{9,8},{10,11... | collective-permute-start | bytes 6291464 | tf_op jit(solution)/shard_map/ppermute | solution.py:217
  398.7 25.0 %collective-permute-start.13 = (bf16[4,512,256]{2,1,0:T(8,128)(2,1)}, bf16[4,512,256]{2,1,0:T(8,128)(2,1)S(1)}, u32[]{:S(2)}, u32[]{:S(2)}) collective-permute-start(bf16[4,512,256]{2,1,0:T(8,128)(2,1)} %get-tuple-element.67), channel_id=1, source_target_pairs={{0,6},{2,4},{4,2},{6,0},{8,14},{10,12},{12,10},{14,8},{16,22},{18,... | collective-permute-start | bytes 3145736 | tf_op jit(solution)/shard_map/ppermute | solution.py:207
  400.0 47.1 %collective-permute-start.12 = (bf16[4,512,256]{2,1,0:T(8,128)(2,1)}, bf16[4,512,256]{2,1,0:T(8,128)(2,1)S(1)}, u32[]{:S(2)}, u32[]{:S(2)}) collective-permute-start(bf16[4,512,256]{2,1,0:T(8,128)(2,1)} %get-tuple-element.66), channel_id=1, source_target_pairs={{0,4},{2,6},{4,0},{6,2},{8,12},{10,14},{12,8},{14,10},{16,20},{18,... | collective-permute-start | bytes 3145736 | tf_op jit(solution)/shard_map/ppermute | solution.py:207
  401.7 45.5 %collective-permute-start.11 = (bf16[4,512,256]{2,1,0:T(8,128)(2,1)}, bf16[4,512,256]{2,1,0:T(8,128)(2,1)S(1)}, u32[]{:S(2)}, u32[]{:S(2)}) collective-permute-start(bf16[4,512,256]{2,1,0:T(8,128)(2,1)} %get-tuple-element.65), channel_id=1, source_target_pairs={{0,2},{2,0},{4,6},{6,4},{8,10},{10,8},{12,14},{14,12},{16,18},{18,... | collective-permute-start | bytes 3145736 | tf_op jit(solution)/shard_map/ppermute | solution.py:207
  401.7 53.9 %collective-permute-start.18 = (bf16[2048,512]{1,0:T(8,128)(2,1)S(1)}, bf16[2048,512]{1,0:T(8,128)(2,1)S(1)}, u32[]{:S(2)}, u32[]{:S(2)}) collective-permute-start(bf16[2048,512]{1,0:T(8,128)(2,1)S(1)} %attend_head.6), channel_id=1, source_target_pairs={{0,1},{1,0},{2,3},{3,2},{4,5},{5,4},{6,7},{7,6},{8,9},{9,8},{10,11... | collective-permute-start | bytes 6291464 | tf_op jit(solution)/shard_map/ppermute | solution.py:217
  401.7 46.2 %slice-start = ((s8[8388608]{0:T(1024)(128)(4,1)}), s8[4194304]{0:T(1024)(128)(4,1)S(1)}, s32[]{:S(2)}) async-start(s8[8388608]{0:T(1024)(128)(4,1)} %bitcast.35), calls=%async_computation.3 | async-start | bytes 8388608
  406.0 41.1 %copy-start.9 = (bf16[4,512,256]{2,1,0:T(8,128)(2,1)S(1)}, bf16[4,512,256]{2,1,0:T(8,128)(2,1)}, u32[]{:S(2)}) copy-start(bf16[4,512,256]{2,1,0:T(8,128)(2,1)} %get-tuple-element.64) | copy-start | bytes 3145732
  406.0 41.9 %slice-start.1 = ((s8[8388608]{0:T(1024)(128)(4,1)}), s8[4194304]{0:T(1024)(128)(4,1)S(1)}, s32[]{:S(2)}) async-start(s8[8388608]{0:T(1024)(128)(4,1)} %bitcast.35), calls=%async_computation.4 | async-start | bytes 8388608
  455.5 8.7 %copy-start.2 = (bf16[2048,512]{1,0:T(8,128)(2,1)S(1)}, bf16[2048,512]{1,0:T(8,128)(2,1)}, u32[]{:S(2)}) copy-start(bf16[2048,512]{1,0:T(8,128)(2,1)} %key_ref.9) | copy-start | bytes 6291460
  455.5 8.7 %copy-start.5 = (bf16[2048,512]{1,0:T(8,128)(2,1)S(1)}, bf16[2048,512]{1,0:T(8,128)(2,1)}, u32[]{:S(2)}) copy-start(bf16[2048,512]{1,0:T(8,128)(2,1)} %value_ref.9) | copy-start | bytes 6291460
  476.9 25.2 %collective-permute-start.20 = (bf16[1024,512]{1,0:T(8,128)(2,1)S(1)}, bf16[1024,512]{1,0:T(8,128)(2,1)S(1)}, u32[]{:S(2)}, u32[]{:S(2)}) collective-permute-start(bf16[1024,512]{1,0:T(8,128)(2,1)S(1)} %attend_head.9), channel_id=1, source_target_pairs={{0,1},{1,0},{2,3},{3,2},{4,5},{5,4},{6,7},{7,6},{8,9},{9,8},{10,11... | collective-permute-start | bytes 3145736 | tf_op jit(solution)/shard_map/ppermute | solution.py:217
  489.9 34.6 %collective-permute-start.19 = (bf16[1024,512]{1,0:T(8,128)(2,1)S(1)}, bf16[1024,512]{1,0:T(8,128)(2,1)S(1)}, u32[]{:S(2)}, u32[]{:S(2)}) collective-permute-start(bf16[1024,512]{1,0:T(8,128)(2,1)S(1)} %attend_head.8), channel_id=1, source_target_pairs={{0,1},{1,0},{2,3},{3,2},{4,5},{5,4},{6,7},{7,6},{8,9},{9,8},{10,11... | collective-permute-start | bytes 3145736 | tf_op jit(solution)/shard_map/ppermute | solution.py:217
Sparse Core Ops, SparseCore 0:
  10.3 98.9 all-gather.9
  110.9 99.2 all-gather.11
  269.4 78.0 all-gather.7
